TPU v7x, 128 devices: a whole 4x4x4 slice. The times are simulated.
128 devices in a mesh: gx: 32 (over y, x, core), gz: 4 (over z).
Axes of the slice: x: 4, y: 4, z: 4, core: 2. Of those that a mesh axis runs over, the one named last changes fastest.
Arguments:
- features: float32 [4, 1024, 128, 512], P(None, 'gx', None, 'gz'), may hold values from -6 to 6
- w_in: float32 [16, 4], replicated, may hold values from -3 to 3
- b_in: float32 [16], replicated, may hold values from -3 to 3
- w_out: float32 [12, 16], replicated, may hold values from -1.5 to 1.5
- b_out: float32 [12], replicated, may hold values from -4 to 4
- band_depth: float32 [8], replicated, may hold values from 0.5 to 20
- band_mix: float32 [3, 8], replicated, may hold values from 0.05 to 0.3
Outputs:
- light: float32 [3, 1024, 128, 512], P(None, 'gx', None, 'gz')
- image: float32 [4, 1024, 128], P(None, 'gx', 'gz')
All inputs are finite; a program needn't handle non-finite values.
Results may differ from a plain program's by a relative error of at most 0.0003.
Values sent between devices are 32-bit elements; how exact they have to be, the bound alone decides.
No kernel may reach another device: no remote copies, remote signals or barrier semaphores. Data moves between devices by JAX's collectives and lax.ppermute only.
A program may use at most 192 MiB of HBM per device.

v0:
```python
import jax
import jax.numpy as jnp
from jax import lax
from jax.sharding import PartitionSpec as P


def shifted(value, axis, steps):
    count = lax.axis_size(axis)
    initial, last = (max(0, -steps), min(count, count - steps))
    return lax.ppermute(value, axis, [(source, source + steps) for source in range(initial, last)])


def partner(shard, axis, apart):
    return lax.ppermute(shard, axis, [(i, i ^ 1 << apart) for i in range(lax.axis_size(axis))])


def body(features, w_in, b_in, w_out, b_out, band_depth, band_mix):
    high = lax.Precision.HIGHEST
    cells_x = features.shape[1]
    rows_y = features.shape[2]
    cells_z = features.shape[3]
    total_x = cells_x * lax.axis_size("gx")
    total_z = cells_z * lax.axis_size("gz")
    bands = band_depth.shape[0]
    hidden = jax.nn.relu(
        jnp.einsum("hc,cxyz->hxyz", w_in, features, precision=high) + b_in[:, None, None, None]
    )
    raw = jnp.einsum("oh,hxyz->oxyz", w_out, hidden, precision=high) + b_out[:, None, None, None]
    extinction = jax.nn.softplus(raw[:bands]) * (band_depth / total_x)[:, None, None, None]
    local_shadow = jnp.cumsum(extinction, axis=1) - extinction
    plane_total = jnp.sum(extinction, axis=1)

    def hand_on(step, incoming):
        return shifted(incoming + plane_total, "gx", 1)

    incoming = lax.fori_loop(0, lax.axis_size("gx") - 1, hand_on, jnp.zeros_like(plane_total))
    shadow = local_shadow + incoming[:, None]
    light = jax.nn.sigmoid(raw[bands : bands + 3]) * jnp.einsum(
        "kb,bxyz->kxyz", band_mix, jnp.exp(-shadow), precision=high
    )
    kappa = jax.nn.softplus(raw[bands + 3]) / total_z
    occlusion = jnp.cumsum(kappa, axis=2) - kappa
    weight = jnp.exp(-occlusion) * (1.0 - jnp.exp(-kappa))
    colour = jnp.sum(light * weight[None], axis=3)
    depth = jnp.sum(kappa, axis=2)
    ndev = lax.axis_size("gz")
    row_share = rows_y // ndev
    levels = ndev.bit_length() - 1
    colour = colour.reshape((3, cells_x) + (2,) * levels + (row_share,))
    depth = depth.reshape((cells_x,) + (2,) * levels + (row_share,))
    me = lax.axis_index("gz")
    for bit in range(levels):
        mine = me >> bit & 1
        other = 1 - mine
        axis_colour = 2 + levels - 1 - bit
        axis_depth = 1 + levels - 1 - bit
        keep_colour = lax.dynamic_index_in_dim(colour, mine, axis_colour, keepdims=False)
        send_colour = lax.dynamic_index_in_dim(colour, other, axis_colour, keepdims=False)
        keep_depth = lax.dynamic_index_in_dim(depth, mine, axis_depth, keepdims=False)
        send_depth = lax.dynamic_index_in_dim(depth, other, axis_depth, keepdims=False)
        got_colour, got_depth = partner((send_colour, send_depth), "gz", bit)
        in_front = keep_colour + jnp.exp(-keep_depth)[None] * got_colour
        behind = got_colour + jnp.exp(-got_depth)[None] * keep_colour
        colour = jnp.where(mine == 0, in_front, behind)
        depth = keep_depth + got_depth
    image = jnp.concatenate([colour, (1.0 - jnp.exp(-depth))[None]], axis=0)
    return (light, image)


def solution(mesh):
    in_specs = (P(None, "gx", None, "gz"), P(), P(), P(), P(), P(), P())
    out_specs = (P(None, "gx", None, "gz"), P(None, "gx", "gz"))
    return jax.shard_map(body, mesh=mesh, in_specs=in_specs, out_specs=out_specs, check_vma=False)
```

profile of v0, /device:TPU:16, one launch (start us, length us, event | category | flops | bytes accessed | tf_op | source)
XLA Modules:
  0.0 603.4 jit_solution(14379119434531477512)
XLA Ops:
  0.7 38.3 %fusion.9 = f32[16,32,128,128]{3,0,2,1:T(8,128)} fusion(f32[4,32,128,128]{3,2,1,0:T(8,128)} %param.9, f32[16,4]{0,1:T(4,128)} %param.10), kind=kOutput, calls=%fused_computation.12 | convolution fusion | flops 402653184 | bytes 41943296 | tf_op jit(solution)/shard_map/hc,cxyz->hxyz/dot_general | solution.py:26
  38.9 37.6 %fusion = f32[32,128,128,12]{2,3,1,0:T(8,128)} fusion(f32[16,32,128,128]{3,0,2,1:T(8,128)} %fusion.9, f32[16]{0:T(128)S(1)} %copy-done.5, f32[12,16]{1,0:T(8,128)S(1)} %copy-done), kind=kOutput, calls=%fused_computation.1 | convolution fusion | flops 1224736768 | bytes 58721088 | tf_op jit(solution)/shard_map/oh,hxyz->oxyz/dot_general | solution.py:28
  76.5 16.9 %fusion.3 = f32[12,32,128,128]{3,2,1,0:T(8,128)S(1)} fusion(f32[32,128,128,12]{2,3,1,0:T(8,128)} %fusion, f32[12]{0:T(128)S(1)} %copy-done.6), kind=kLoop, calls=%fused_computation.5 | loop fusion | flops 6291456 | bytes 50331696 | tf_op jit(solution)/shard_map/add | solution.py:28
  120.2 12.0 %fusion.26 = f32[8,128,128]{2,1,0:T(8,128)S(1)} fusion(f32[8]{0:T(128)S(1)} %broadcast_multiply_fusion, f32[12,32,128,128]{3,2,1,0:T(8,128)} %copy-done.2), kind=kLoop, calls=%fused_computation.53 | loop fusion | flops 33423360 | bytes 17301536 | tf_op jit(solution)/shard_map/reduce_sum | solution.py:31
  132.2 392.8 %while.10 = (s32[]{:T(128)}, f32[8,128,128]{2,1,0:T(8,128)S(1)}, f32[8,128,128]{2,1,0:T(8,128)S(1)}, s32[]{:T(128)}) while((s32[]{:T(128)}, f32[8,128,128]{2,1,0:T(8,128)S(1)}, f32[8,128,128]{2,1,0:T(8,128)S(1)}, s32[]{:T(128)}) %tuple.37), condition=%wide.region_3.4_spmd, body=%wide.region_2.3_spmd.sunk | while | flops 131074 | bytes 3670109 | solution.py:36
  134.3 10.7 %collective-permute-done = f32[8,128,128]{2,1,0:T(8,128)S(1)} collective-permute-done((f32[8,128,128]{2,1,0:T(8,128)S(1)}, f32[8,128,128]{2,1,0:T(8,128)S(1)}, u32[]{:S(2)}, u32[]{:S(2)}) %collective-permute-start) | collective-permute-done | bytes 524320 | tf_op jit(solution)/shard_map/while/body/eval_jaxpr/ppermute | solution.py:10
  146.9 10.7 %collective-permute-done = f32[8,128,128]{2,1,0:T(8,128)S(1)} collective-permute-done((f32[8,128,128]{2,1,0:T(8,128)S(1)}, f32[8,128,128]{2,1,0:T(8,128)S(1)}, u32[]{:S(2)}, u32[]{:S(2)}) %collective-permute-start) | collective-permute-done | bytes 524320 | tf_op jit(solution)/shard_map/while/body/eval_jaxpr/ppermute | solution.py:10
  159.6 10.7 %collective-permute-done = f32[8,128,128]{2,1,0:T(8,128)S(1)} collective-permute-done((f32[8,128,128]{2,1,0:T(8,128)S(1)}, f32[8,128,128]{2,1,0:T(8,128)S(1)}, u32[]{:S(2)}, u32[]{:S(2)}) %collective-permute-start) | collective-permute-done | bytes 524320 | tf_op jit(solution)/shard_map/while/body/eval_jaxpr/ppermute | solution.py:10
  172.3 10.7 %collective-permute-done = f32[8,128,128]{2,1,0:T(8,128)S(1)} collective-permute-done((f32[8,128,128]{2,1,0:T(8,128)S(1)}, f32[8,128,128]{2,1,0:T(8,128)S(1)}, u32[]{:S(2)}, u32[]{:S(2)}) %collective-permute-start) | collective-permute-done | bytes 524320 | tf_op jit(solution)/shard_map/while/body/eval_jaxpr/ppermute | solution.py:10
  184.9 10.7 %collective-permute-done = f32[8,128,128]{2,1,0:T(8,128)S(1)} collective-permute-done((f32[8,128,128]{2,1,0:T(8,128)S(1)}, f32[8,128,128]{2,1,0:T(8,128)S(1)}, u32[]{:S(2)}, u32[]{:S(2)}) %collective-permute-start) | collective-permute-done | bytes 524320 | tf_op jit(solution)/shard_map/while/body/eval_jaxpr/ppermute | solution.py:10
  197.6 10.7 %collective-permute-done = f32[8,128,128]{2,1,0:T(8,128)S(1)} collective-permute-done((f32[8,128,128]{2,1,0:T(8,128)S(1)}, f32[8,128,128]{2,1,0:T(8,128)S(1)}, u32[]{:S(2)}, u32[]{:S(2)}) %collective-permute-start) | collective-permute-done | bytes 524320 | tf_op jit(solution)/shard_map/while/body/eval_jaxpr/ppermute | solution.py:10
  210.3 10.7 %collective-permute-done = f32[8,128,128]{2,1,0:T(8,128)S(1)} collective-permute-done((f32[8,128,128]{2,1,0:T(8,128)S(1)}, f32[8,128,128]{2,1,0:T(8,128)S(1)}, u32[]{:S(2)}, u32[]{:S(2)}) %collective-permute-start) | collective-permute-done | bytes 524320 | tf_op jit(solution)/shard_map/while/body/eval_jaxpr/ppermute | solution.py:10
  222.9 10.7 %collective-permute-done = f32[8,128,128]{2,1,0:T(8,128)S(1)} collective-permute-done((f32[8,128,128]{2,1,0:T(8,128)S(1)}, f32[8,128,128]{2,1,0:T(8,128)S(1)}, u32[]{:S(2)}, u32[]{:S(2)}) %collective-permute-start) | collective-permute-done | bytes 524320 | tf_op jit(solution)/shard_map/while/body/eval_jaxpr/ppermute | solution.py:10
  235.6 10.7 %collective-permute-done = f32[8,128,128]{2,1,0:T(8,128)S(1)} collective-permute-done((f32[8,128,128]{2,1,0:T(8,128)S(1)}, f32[8,128,128]{2,1,0:T(8,128)S(1)}, u32[]{:S(2)}, u32[]{:S(2)}) %collective-permute-start) | collective-permute-done | bytes 524320 | tf_op jit(solution)/shard_map/while/body/eval_jaxpr/ppermute | solution.py:10
  248.3 10.7 %collective-permute-done = f32[8,128,128]{2,1,0:T(8,128)S(1)} collective-permute-done((f32[8,128,128]{2,1,0:T(8,128)S(1)}, f32[8,128,128]{2,1,0:T(8,128)S(1)}, u32[]{:S(2)}, u32[]{:S(2)}) %collective-permute-start) | collective-permute-done | bytes 524320 | tf_op jit(solution)/shard_map/while/body/eval_jaxpr/ppermute | solution.py:10
  261.0 10.7 %collective-permute-done = f32[8,128,128]{2,1,0:T(8,128)S(1)} collective-permute-done((f32[8,128,128]{2,1,0:T(8,128)S(1)}, f32[8,128,128]{2,1,0:T(8,128)S(1)}, u32[]{:S(2)}, u32[]{:S(2)}) %collective-permute-start) | collective-permute-done | bytes 524320 | tf_op jit(solution)/shard_map/while/body/eval_jaxpr/ppermute | solution.py:10
  273.6 10.7 %collective-permute-done = f32[8,128,128]{2,1,0:T(8,128)S(1)} collective-permute-done((f32[8,128,128]{2,1,0:T(8,128)S(1)}, f32[8,128,128]{2,1,0:T(8,128)S(1)}, u32[]{:S(2)}, u32[]{:S(2)}) %collective-permute-start) | collective-permute-done | bytes 524320 | tf_op jit(solution)/shard_map/while/body/eval_jaxpr/ppermute | solution.py:10
  286.3 10.7 %collective-permute-done = f32[8,128,128]{2,1,0:T(8,128)S(1)} collective-permute-done((f32[8,128,128]{2,1,0:T(8,128)S(1)}, f32[8,128,128]{2,1,0:T(8,128)S(1)}, u32[]{:S(2)}, u32[]{:S(2)}) %collective-permute-start) | collective-permute-done | bytes 524320 | tf_op jit(solution)/shard_map/while/body/eval_jaxpr/ppermute | solution.py:10
  299.0 10.7 %collective-permute-done = f32[8,128,128]{2,1,0:T(8,128)S(1)} collective-permute-done((f32[8,128,128]{2,1,0:T(8,128)S(1)}, f32[8,128,128]{2,1,0:T(8,128)S(1)}, u32[]{:S(2)}, u32[]{:S(2)}) %collective-permute-start) | collective-permute-done | bytes 524320 | tf_op jit(solution)/shard_map/while/body/eval_jaxpr/ppermute | solution.py:10
  311.6 10.7 %collective-permute-done = f32[8,128,128]{2,1,0:T(8,128)S(1)} collective-permute-done((f32[8,128,128]{2,1,0:T(8,128)S(1)}, f32[8,128,128]{2,1,0:T(8,128)S(1)}, u32[]{:S(2)}, u32[]{:S(2)}) %collective-permute-start) | collective-permute-done | bytes 524320 | tf_op jit(solution)/shard_map/while/body/eval_jaxpr/ppermute | solution.py:10
  324.3 10.7 %collective-permute-done = f32[8,128,128]{2,1,0:T(8,128)S(1)} collective-permute-done((f32[8,128,128]{2,1,0:T(8,128)S(1)}, f32[8,128,128]{2,1,0:T(8,128)S(1)}, u32[]{:S(2)}, u32[]{:S(2)}) %collective-permute-start) | collective-permute-done | bytes 524320 | tf_op jit(solution)/shard_map/while/body/eval_jaxpr/ppermute | solution.py:10
  337.0 10.7 %collective-permute-done = f32[8,128,128]{2,1,0:T(8,128)S(1)} collective-permute-done((f32[8,128,128]{2,1,0:T(8,128)S(1)}, f32[8,128,128]{2,1,0:T(8,128)S(1)}, u32[]{:S(2)}, u32[]{:S(2)}) %collective-permute-start) | collective-permute-done | bytes 524320 | tf_op jit(solution)/shard_map/while/body/eval_jaxpr/ppermute | solution.py:10
  525.0 28.7 %negate_exponential_fusion = f32[8,32,128,128]{3,2,1,0:T(8,128)} fusion(f32[8,128,128]{2,1,0:T(8,128)S(1)} %get-tuple-element.19, f32[8]{0:T(128)S(1)} %broadcast_multiply_fusion, f32[12,32,128,128]{3,2,1,0:T(8,128)} %copy-done.2), kind=kOutput, calls=%fused_computation.9 | output fusion | flops 201326592 | bytes 50856960 | tf_op jit(solution)/shard_map/jit(cumsum)/reduce_window_sum | solution.py:30
  553.7 29.0 %fusion.5 = f32[32,128,128,3]{2,3,1,0:T(4,128)S(1)} fusion(f32[8,32,128,128]{3,2,1,0:T(8,128)} %negate_exponential_fusion, f32[3,8]{1,0:T(4,128)S(1)} %copy-done.4), kind=kOutput, calls=%fused_computation.7 | convolution fusion | flops 150994944 | bytes 23068768 | tf_op jit(solution)/shard_map/kb,bxyz->kxyz/dot_general | solution.py:38
  (122 shorter events, 257.9 us)
Async XLA Ops:
  103.3 489.4 %collective-permute-start.2 = (f32[32,2,32]{2,1,0:T(2,128)S(1)}, f32[32,2,32]{2,1,0:T(2,128)S(1)}, u32[]{:S(2)}, u32[]{:S(2)}) collective-permute-start(f32[32,2,32]{2,1,0:T(2,128)S(1)} %bitcast.71), channel_id=1, source_target_pairs={{0,1},{1,0},{2,3},{3,2},{4,5},{5,4},{6,7},{7,6},{8,9},{9,8},{10,11... | collective-permute-start | bytes 24584 | tf_op jit(solution)/shard_map/ppermute | solution.py:14
  132.3 12.6 %collective-permute-start = (f32[8,128,128]{2,1,0:T(8,128)S(1)}, f32[8,128,128]{2,1,0:T(8,128)S(1)}, u32[]{:S(2)}, u32[]{:S(2)}) collective-permute-start(f32[8,128,128]{2,1,0:T(8,128)S(1)} %add.152), channel_id=1, source_target_pairs={{0,4},{4,8},{8,12},{12,16},{16,20},{20,24},{24,28},{28,32},{32,36}... | collective-permute-start | bytes 1572872 | tf_op jit(solution)/shard_map/while/body/eval_jaxpr/ppermute | solution.py:10
  145.0 12.6 %collective-permute-start = (f32[8,128,128]{2,1,0:T(8,128)S(1)}, f32[8,128,128]{2,1,0:T(8,128)S(1)}, u32[]{:S(2)}, u32[]{:S(2)}) collective-permute-start(f32[8,128,128]{2,1,0:T(8,128)S(1)} %add.152), channel_id=1, source_target_pairs={{0,4},{4,8},{8,12},{12,16},{16,20},{20,24},{24,28},{28,32},{32,36}... | collective-permute-start | bytes 1572872 | tf_op jit(solution)/shard_map/while/body/eval_jaxpr/ppermute | solution.py:10
  157.7 12.6 %collective-permute-start = (f32[8,128,128]{2,1,0:T(8,128)S(1)}, f32[8,128,128]{2,1,0:T(8,128)S(1)}, u32[]{:S(2)}, u32[]{:S(2)}) collective-permute-start(f32[8,128,128]{2,1,0:T(8,128)S(1)} %add.152), channel_id=1, source_target_pairs={{0,4},{4,8},{8,12},{12,16},{16,20},{20,24},{24,28},{28,32},{32,36}... | collective-permute-start | bytes 1572872 | tf_op jit(solution)/shard_map/while/body/eval_jaxpr/ppermute | solution.py:10
  170.3 12.6 %collective-permute-start = (f32[8,128,128]{2,1,0:T(8,128)S(1)}, f32[8,128,128]{2,1,0:T(8,128)S(1)}, u32[]{:S(2)}, u32[]{:S(2)}) collective-permute-start(f32[8,128,128]{2,1,0:T(8,128)S(1)} %add.152), channel_id=1, source_target_pairs={{0,4},{4,8},{8,12},{12,16},{16,20},{20,24},{24,28},{28,32},{32,36}... | collective-permute-start | bytes 1572872 | tf_op jit(solution)/shard_map/while/body/eval_jaxpr/ppermute | solution.py:10
  183.0 12.6 %collective-permute-start = (f32[8,128,128]{2,1,0:T(8,128)S(1)}, f32[8,128,128]{2,1,0:T(8,128)S(1)}, u32[]{:S(2)}, u32[]{:S(2)}) collective-permute-start(f32[8,128,128]{2,1,0:T(8,128)S(1)} %add.152), channel_id=1, source_target_pairs={{0,4},{4,8},{8,12},{12,16},{16,20},{20,24},{24,28},{28,32},{32,36}... | collective-permute-start | bytes 1572872 | tf_op jit(solution)/shard_map/while/body/eval_jaxpr/ppermute | solution.py:10
  195.7 12.6 %collective-permute-start = (f32[8,128,128]{2,1,0:T(8,128)S(1)}, f32[8,128,128]{2,1,0:T(8,128)S(1)}, u32[]{:S(2)}, u32[]{:S(2)}) collective-permute-start(f32[8,128,128]{2,1,0:T(8,128)S(1)} %add.152), channel_id=1, source_target_pairs={{0,4},{4,8},{8,12},{12,16},{16,20},{20,24},{24,28},{28,32},{32,36}... | collective-permute-start | bytes 1572872 | tf_op jit(solution)/shard_map/while/body/eval_jaxpr/ppermute | solution.py:10
  208.3 12.6 %collective-permute-start = (f32[8,128,128]{2,1,0:T(8,128)S(1)}, f32[8,128,128]{2,1,0:T(8,128)S(1)}, u32[]{:S(2)}, u32[]{:S(2)}) collective-permute-start(f32[8,128,128]{2,1,0:T(8,128)S(1)} %add.152), channel_id=1, source_target_pairs={{0,4},{4,8},{8,12},{12,16},{16,20},{20,24},{24,28},{28,32},{32,36}... | collective-permute-start | bytes 1572872 | tf_op jit(solution)/shard_map/while/body/eval_jaxpr/ppermute | solution.py:10
  221.0 12.6 %collective-permute-start = (f32[8,128,128]{2,1,0:T(8,128)S(1)}, f32[8,128,128]{2,1,0:T(8,128)S(1)}, u32[]{:S(2)}, u32[]{:S(2)}) collective-permute-start(f32[8,128,128]{2,1,0:T(8,128)S(1)} %add.152), channel_id=1, source_target_pairs={{0,4},{4,8},{8,12},{12,16},{16,20},{20,24},{24,28},{28,32},{32,36}... | collective-permute-start | bytes 1572872 | tf_op jit(solution)/shard_map/while/body/eval_jaxpr/ppermute | solution.py:10
  233.7 12.6 %collective-permute-start = (f32[8,128,128]{2,1,0:T(8,128)S(1)}, f32[8,128,128]{2,1,0:T(8,128)S(1)}, u32[]{:S(2)}, u32[]{:S(2)}) collective-permute-start(f32[8,128,128]{2,1,0:T(8,128)S(1)} %add.152), channel_id=1, source_target_pairs={{0,4},{4,8},{8,12},{12,16},{16,20},{20,24},{24,28},{28,32},{32,36}... | collective-permute-start | bytes 1572872 | tf_op jit(solution)/shard_map/while/body/eval_jaxpr/ppermute | solution.py:10
  246.4 12.6 %collective-permute-start = (f32[8,128,128]{2,1,0:T(8,128)S(1)}, f32[8,128,128]{2,1,0:T(8,128)S(1)}, u32[]{:S(2)}, u32[]{:S(2)}) collective-permute-start(f32[8,128,128]{2,1,0:T(8,128)S(1)} %add.152), channel_id=1, source_target_pairs={{0,4},{4,8},{8,12},{12,16},{16,20},{20,24},{24,28},{28,32},{32,36}... | collective-permute-start | bytes 1572872 | tf_op jit(solution)/shard_map/while/body/eval_jaxpr/ppermute | solution.py:10
  259.0 12.6 %collective-permute-start = (f32[8,128,128]{2,1,0:T(8,128)S(1)}, f32[8,128,128]{2,1,0:T(8,128)S(1)}, u32[]{:S(2)}, u32[]{:S(2)}) collective-permute-start(f32[8,128,128]{2,1,0:T(8,128)S(1)} %add.152), channel_id=1, source_target_pairs={{0,4},{4,8},{8,12},{12,16},{16,20},{20,24},{24,28},{28,32},{32,36}... | collective-permute-start | bytes 1572872 | tf_op jit(solution)/shard_map/while/body/eval_jaxpr/ppermute | solution.py:10
  271.7 12.6 %collective-permute-start = (f32[8,128,128]{2,1,0:T(8,128)S(1)}, f32[8,128,128]{2,1,0:T(8,128)S(1)}, u32[]{:S(2)}, u32[]{:S(2)}) collective-permute-start(f32[8,128,128]{2,1,0:T(8,128)S(1)} %add.152), channel_id=1, source_target_pairs={{0,4},{4,8},{8,12},{12,16},{16,20},{20,24},{24,28},{28,32},{32,36}... | collective-permute-start | bytes 1572872 | tf_op jit(solution)/shard_map/while/body/eval_jaxpr/ppermute | solution.py:10
  284.4 12.6 %collective-permute-start = (f32[8,128,128]{2,1,0:T(8,128)S(1)}, f32[8,128,128]{2,1,0:T(8,128)S(1)}, u32[]{:S(2)}, u32[]{:S(2)}) collective-permute-start(f32[8,128,128]{2,1,0:T(8,128)S(1)} %add.152), channel_id=1, source_target_pairs={{0,4},{4,8},{8,12},{12,16},{16,20},{20,24},{24,28},{28,32},{32,36}... | collective-permute-start | bytes 1572872 | tf_op jit(solution)/shard_map/while/body/eval_jaxpr/ppermute | solution.py:10
  297.0 12.6 %collective-permute-start = (f32[8,128,128]{2,1,0:T(8,128)S(1)}, f32[8,128,128]{2,1,0:T(8,128)S(1)}, u32[]{:S(2)}, u32[]{:S(2)}) collective-permute-start(f32[8,128,128]{2,1,0:T(8,128)S(1)} %add.152), channel_id=1, source_target_pairs={{0,4},{4,8},{8,12},{12,16},{16,20},{20,24},{24,28},{28,32},{32,36}... | collective-permute-start | bytes 1572872 | tf_op jit(solution)/shard_map/while/body/eval_jaxpr/ppermute | solution.py:10
  309.7 12.6 %collective-permute-start = (f32[8,128,128]{2,1,0:T(8,128)S(1)}, f32[8,128,128]{2,1,0:T(8,128)S(1)}, u32[]{:S(2)}, u32[]{:S(2)}) collective-permute-start(f32[8,128,128]{2,1,0:T(8,128)S(1)} %add.152), channel_id=1, source_target_pairs={{0,4},{4,8},{8,12},{12,16},{16,20},{20,24},{24,28},{28,32},{32,36}... | collective-permute-start | bytes 1572872 | tf_op jit(solution)/shard_map/while/body/eval_jaxpr/ppermute | solution.py:10
  322.4 12.6 %collective-permute-start = (f32[8,128,128]{2,1,0:T(8,128)S(1)}, f32[8,128,128]{2,1,0:T(8,128)S(1)}, u32[]{:S(2)}, u32[]{:S(2)}) collective-permute-start(f32[8,128,128]{2,1,0:T(8,128)S(1)} %add.152), channel_id=1, source_target_pairs={{0,4},{4,8},{8,12},{12,16},{16,20},{20,24},{24,28},{28,32},{32,36}... | collective-permute-start | bytes 1572872 | tf_op jit(solution)/shard_map/while/body/eval_jaxpr/ppermute | solution.py:10
  335.0 12.6 %collective-permute-start = (f32[8,128,128]{2,1,0:T(8,128)S(1)}, f32[8,128,128]{2,1,0:T(8,128)S(1)}, u32[]{:S(2)}, u32[]{:S(2)}) collective-permute-start(f32[8,128,128]{2,1,0:T(8,128)S(1)} %add.152), channel_id=1, source_target_pairs={{0,4},{4,8},{8,12},{12,16},{16,20},{20,24},{24,28},{28,32},{32,36}... | collective-permute-start | bytes 1572872 | tf_op jit(solution)/shard_map/while/body/eval_jaxpr/ppermute | solution.py:10
  347.7 12.6 %collective-permute-start = (f32[8,128,128]{2,1,0:T(8,128)S(1)}, f32[8,128,128]{2,1,0:T(8,128)S(1)}, u32[]{:S(2)}, u32[]{:S(2)}) collective-permute-start(f32[8,128,128]{2,1,0:T(8,128)S(1)} %add.152), channel_id=1, source_target_pairs={{0,4},{4,8},{8,12},{12,16},{16,20},{20,24},{24,28},{28,32},{32,36}... | collective-permute-start | bytes 1572872 | tf_op jit(solution)/shard_map/while/body/eval_jaxpr/ppermute | solution.py:10
  360.4 12.6 %collective-permute-start = (f32[8,128,128]{2,1,0:T(8,128)S(1)}, f32[8,128,128]{2,1,0:T(8,128)S(1)}, u32[]{:S(2)}, u32[]{:S(2)}) collective-permute-start(f32[8,128,128]{2,1,0:T(8,128)S(1)} %add.152), channel_id=1, source_target_pairs={{0,4},{4,8},{8,12},{12,16},{16,20},{20,24},{24,28},{28,32},{32,36}... | collective-permute-start | bytes 1572872 | tf_op jit(solution)/shard_map/while/body/eval_jaxpr/ppermute | solution.py:10
  373.1 12.6 %collective-permute-start = (f32[8,128,128]{2,1,0:T(8,128)S(1)}, f32[8,128,128]{2,1,0:T(8,128)S(1)}, u32[]{:S(2)}, u32[]{:S(2)}) collective-permute-start(f32[8,128,128]{2,1,0:T(8,128)S(1)} %add.152), channel_id=1, source_target_pairs={{0,4},{4,8},{8,12},{12,16},{16,20},{20,24},{24,28},{28,32},{32,36}... | collective-permute-start | bytes 1572872 | tf_op jit(solution)/shard_map/while/body/eval_jaxpr/ppermute | solution.py:10
  385.7 12.6 %collective-permute-start = (f32[8,128,128]{2,1,0:T(8,128)S(1)}, f32[8,128,128]{2,1,0:T(8,128)S(1)}, u32[]{:S(2)}, u32[]{:S(2)}) collective-permute-start(f32[8,128,128]{2,1,0:T(8,128)S(1)} %add.152), channel_id=1, source_target_pairs={{0,4},{4,8},{8,12},{12,16},{16,20},{20,24},{24,28},{28,32},{32,36}... | collective-permute-start | bytes 1572872 | tf_op jit(solution)/shard_map/while/body/eval_jaxpr/ppermute | solution.py:10
  398.4 12.6 %collective-permute-start = (f32[8,128,128]{2,1,0:T(8,128)S(1)}, f32[8,128,128]{2,1,0:T(8,128)S(1)}, u32[]{:S(2)}, u32[]{:S(2)}) collective-permute-start(f32[8,128,128]{2,1,0:T(8,128)S(1)} %add.152), channel_id=1, source_target_pairs={{0,4},{4,8},{8,12},{12,16},{16,20},{20,24},{24,28},{28,32},{32,36}... | collective-permute-start | bytes 1572872 | tf_op jit(solution)/shard_map/while/body/eval_jaxpr/ppermute | solution.py:10
  411.1 12.6 %collective-permute-start = (f32[8,128,128]{2,1,0:T(8,128)S(1)}, f32[8,128,128]{2,1,0:T(8,128)S(1)}, u32[]{:S(2)}, u32[]{:S(2)}) collective-permute-start(f32[8,128,128]{2,1,0:T(8,128)S(1)} %add.152), channel_id=1, source_target_pairs={{0,4},{4,8},{8,12},{12,16},{16,20},{20,24},{24,28},{28,32},{32,36}... | collective-permute-start | bytes 1572872 | tf_op jit(solution)/shard_map/while/body/eval_jaxpr/ppermute | solution.py:10
  (19 other events, 329.5 us)
where the time goes:
time: 611 us; the launch traced here: 603 us
  waiting for transfers between devices  333 us (55%)
  matrix products  105 us (17%)
  other arithmetic  77.7 us (13%)
  starting transfers between devices  69.7 us (11%)
  local copies, waits for them, and re-layouts  16.6 us (3%)
    ppermute x31, waiting for transfers between devices, shifted(): lax.ppermute(value, axis, [(source, source + steps) for source in range(i...  331 us
    ppermute x31, starting transfers between devices, shifted(): lax.ppermute(value, axis, [(source, source + steps) for source in range(i...  59.5 us
    dot_general x1, matrix products, body(): jnp.einsum('hc,cxyz->hxyz', w_in, features, precision=high)  38.3 us
    dot_general x1, matrix products, body(): jnp.einsum('oh,hxyz->oxyz', w_out, hidden, precision=high)  37.6 us
    dot_general x1, matrix products, body(): jnp.einsum('kb,bxyz->kxyz', band_mix, jnp.exp(-shadow), precision=high)  29 us
    another operation x1, other arithmetic, body(): local_shadow = jnp.cumsum(extinction, axis=1) - extinction  28.7 us
    add x1, other arithmetic, body(): jnp.einsum('oh,hxyz->oxyz', w_out, hidden, precision=high)  16.9 us
  transfers between devices with their start and end apart: 35, of which 32 were waited for; matrix products, arithmetic and copies ran while one was open for 16% of the time, Pallas kernels for 0%

commit v1 on v0

v1 whole, which is shorter than its diff:
```python
import functools
import math

import jax
import jax.numpy as jnp
from jax import lax
from jax.experimental import pallas as pl
from jax.experimental.pallas import tpu as pltpu
from jax.sharding import PartitionSpec as P

BANDS = 8
UNITS = 16
FEATS = 4
OUTS = 12
SLAB = 16
LOG2E = math.log2(math.e)
F32 = jnp.float32
BF16 = jnp.bfloat16


def iota(shape, dim):
    return lax.broadcasted_iota(jnp.int32, shape, dim)


def split(value):
    high = value.astype(BF16)
    return high, (value - high.astype(F32)).astype(BF16)


def exact_dot(a, b):
    return jnp.dot(a, b, precision=lax.Precision.HIGHEST, preferred_element_type=F32)


def one_hot(shape, condition):
    return jnp.where(condition, jnp.ones(shape, F32), jnp.zeros(shape, F32))


def bias_columns(column):
    rows = column.shape[0]
    high = column.astype(BF16).astype(F32)
    rest = column - high
    middle = rest.astype(BF16).astype(F32)
    low = rest - middle
    lane = iota((rows, 16), 1)
    zero = jnp.zeros((rows, 16), F32)
    return jnp.where(
        lane == 0, high, jnp.where(lane == 1, middle, jnp.where(lane == 2, low, zero))
    ).astype(BF16)


def build_first(w_in, b_in):
    rows, cols = SLAB * UNITS, FEATS * SLAB
    pick = one_hot((rows, UNITS), iota((rows, UNITS), 0) % UNITS == iota((rows, UNITS), 1))
    spread = one_hot((FEATS, cols), iota((FEATS, cols), 1) // SLAB == iota((FEATS, cols), 0))
    full = exact_dot(exact_dot(pick, w_in), spread)
    full = jnp.where(iota((rows, cols), 0) // UNITS == iota((rows, cols), 1) % SLAB, full, 0.0)
    high, low = split(full)
    bias = bias_columns(jnp.sum(pick * b_in, axis=1, keepdims=True))
    return high, low, bias


def build_second(w_out, b_out):
    rows, cols = OUTS * 8, 8 * UNITS
    pick = one_hot((rows, OUTS), iota((rows, OUTS), 0) // 8 == iota((rows, OUTS), 1))
    spread = one_hot((UNITS, cols), iota((UNITS, cols), 1) % UNITS == iota((UNITS, cols), 0))
    full = exact_dot(exact_dot(pick, w_out), spread)
    full = jnp.where(iota((rows, cols), 0) % 8 == iota((rows, cols), 1) // UNITS, full, 0.0)
    out = iota((rows, 1), 0) // 8
    scale = jnp.where((out >= BANDS) & (out < BANDS + 3), -LOG2E, 1.0)
    high, low = split(full * scale)
    bias = bias_columns(jnp.sum(pick * b_out, axis=1, keepdims=True) * scale)
    return high, low, bias


def softplus(x):
    return jnp.maximum(jnp.log(1.0 + jnp.exp(jnp.minimum(x, 80.0))), x)


def front_kernel(total_x, total_z, unroll, f_ref, win_ref, bin_ref, wout_ref, bout_ref, depth_ref,
                 mid_ref, sum_ref, dep_ref, first_ref, second_ref, tri_ref, kap_ref):
    cells_x = f_ref.shape[1]
    step = pl.program_id(0)

    @pl.when(step == 0)
    def _():
        high, low, bias = build_first(win_ref[...], bin_ref[...])
        first_ref[:, 0:64] = high
        first_ref[:, 64:128] = high
        first_ref[:, 128:192] = low
        first_ref[:, 192:208] = bias
        high, low, bias = build_second(wout_ref[...], bout_ref[...])
        second_ref[:, 0:128] = high
        second_ref[:, 128:256] = high
        second_ref[:, 256:384] = low
        second_ref[:, 384:400] = bias
        tri_ref[...] = one_hot((256, 128), iota((256, 128), 0) % 128 < iota((256, 128), 1)).astype(BF16)

    ones = jnp.ones((16, 256), BF16)
    rates = [depth_ref[b] * (-LOG2E / total_x) for b in range(BANDS)]
    fade = -LOG2E / total_z
    y0 = pl.multiple_of(step * SLAB, SLAB)

    def pair(i, sums):
        sums = list(sums)
        x0 = 2 * i
        rows = jnp.concatenate(
            [jnp.concatenate([f_ref[c, x0], f_ref[c, x0 + 1]], axis=1) for c in range(FEATS)], axis=0
        )
        high, low = split(rows)
        hidden = jnp.dot(first_ref[...], jnp.concatenate([high, low, high, ones], axis=0),
                         preferred_element_type=F32)
        high, low = split(jnp.maximum(hidden, 0.0))
        for j in range(2):
            part = slice(j * 128, j * 128 + 128)
            raw = jnp.dot(second_ref[...],
                          jnp.concatenate([high[part], low[part], high[part], ones], axis=0),
                          preferred_element_type=F32)
            here = pl.ds(pl.multiple_of(y0 + 8 * j, 8), 8)
            for s in range(2):
                x = x0 + s
                tile = raw[:, s * 128 : s * 128 + 128]
                for b in range(BANDS):
                    total = sums[j * BANDS + b]
                    mid_ref[b, x, here, :] = jnp.exp2(total * rates[b])
                    sums[j * BANDS + b] = total + softplus(tile[8 * b : 8 * b + 8])
                for k in range(BANDS, BANDS + 3):
                    mid_ref[k, x, here, :] = pl.reciprocal(
                        1.0 + jnp.exp2(tile[8 * k : 8 * k + 8]), approx=True)
                kappa = softplus(tile[8 * BANDS + 24 : 8 * BANDS + 32])
                high_k, low_k = split(kappa)
                both = jnp.concatenate([high_k, low_k], axis=1)
                occlusion = jnp.dot(both, tri_ref[...], preferred_element_type=F32)
                mid_ref[BANDS + 3, x, here, :] = jnp.exp2(occlusion * fade) * (1.0 - jnp.exp2(kappa * fade))
                kap_ref[j, pl.ds(pl.multiple_of(x * 8, 8), 8), :] = jnp.concatenate(
                    [high_k.astype(F32), low_k.astype(F32)], axis=1)
        return tuple(sums)

    zero = jnp.zeros((8, 128), F32)
    sums = lax.fori_loop(0, cells_x // 2, pair, (zero,) * (2 * BANDS), unroll=unroll)
    for j in range(2):
        for b in range(BANDS):
            sum_ref[b, 8 * j : 8 * j + 8, :] = sums[j * BANDS + b]
        select = one_hot((8, 256), iota((8, 256), 0) == 3).astype(BF16)
        dep_ref[j] = lax.dot_general(select, kap_ref[j].astype(BF16), (((1,), (1,)), ((), ())),
                                     preferred_element_type=F32) * (1.0 / total_z)


def back_kernel(total_x, unroll, mid_ref, inc_ref, dep_ref, depth_ref, mix_ref,
                light_ref, img_ref, prod_ref):
    cells_x = light_ref.shape[1]
    gains = []
    for b in range(BANDS):
        fade = jnp.exp2(inc_ref[b] * (depth_ref[b] * (-LOG2E / total_x)))
        gains.append([fade * mix_ref[k * BANDS + b] for k in range(3)])

    def one(x, carry):
        bands = [mid_ref[b, x] for b in range(BANDS)]
        weight = mid_ref[BANDS + 3, x]
        for k in range(3):
            total = bands[0] * gains[0][k]
            for b in range(1, BANDS):
                total = total + bands[b] * gains[b][k]
            light = total * mid_ref[BANDS + k, x]
            light_ref[k, x] = light
            high, low = split(light * weight)
            here = pl.ds(pl.multiple_of(x * 8, 8), 8)
            prod_ref[here, 256 * k : 256 * k + 128] = high.astype(F32)
            prod_ref[here, 256 * k + 128 : 256 * k + 256] = low.astype(F32)
        return carry

    lax.fori_loop(0, cells_x, one, 0, unroll=unroll)
    select = one_hot((8, 768), iota((8, 768), 0) == iota((8, 768), 1) // 256).astype(BF16)
    img_ref[0] = lax.dot_general(select, prod_ref[...].astype(BF16), (((1,), (1,)), ((), ())),
                                 preferred_element_type=F32) + dep_ref[0]


def front(features, w_in, b_in, w_out, b_out, band_depth, total_x, total_z):
    _, cells_x, rows_y, cells_z = features.shape
    whole = pl.BlockSpec(memory_space=pltpu.VMEM)
    return pl.pallas_call(
        functools.partial(front_kernel, total_x, total_z, 2),
        grid=(rows_y // SLAB,),
        in_specs=[
            pl.BlockSpec((FEATS, cells_x, SLAB, cells_z), lambda i: (0, 0, i, 0)),
            whole, whole, whole, whole,
            pl.BlockSpec(memory_space=pltpu.SMEM),
        ],
        out_specs=[
            whole,
            pl.BlockSpec((BANDS, SLAB, cells_z), lambda i: (0, i, 0)),
            pl.BlockSpec((2, 8, 256), lambda i: (i, 0, 0)),
        ],
        out_shape=[
            pltpu.MemorySpace.VMEM((OUTS, cells_x, rows_y, cells_z), F32),
            jax.ShapeDtypeStruct((BANDS, rows_y, cells_z), F32),
            jax.ShapeDtypeStruct((rows_y // 8, 8, 256), F32),
        ],
        scratch_shapes=[
            pltpu.VMEM((SLAB * UNITS, 208), BF16),
            pltpu.VMEM((OUTS * 8, 400), BF16),
            pltpu.VMEM((256, 128), BF16),
            pltpu.VMEM((2, 256, 256), F32),
        ],
        compiler_params=pltpu.CompilerParams(vmem_limit_bytes=24 << 20),
        name="front",
    )(features, w_in, b_in[None], w_out, b_out[None], band_depth)


def back(mid, incoming, dep, band_depth, band_mix, total_x):
    _, cells_x, rows_y, cells_z = mid.shape
    return pl.pallas_call(
        functools.partial(back_kernel, total_x, 4),
        grid=(rows_y // 8,),
        in_specs=[
            pl.BlockSpec((OUTS, cells_x, 8, cells_z), lambda i: (0, 0, i, 0)),
            pl.BlockSpec((BANDS, 8, cells_z), lambda i: (0, i, 0)),
            pl.BlockSpec((1, 8, 256), lambda i: (i, 0, 0)),
            pl.BlockSpec(memory_space=pltpu.SMEM),
            pl.BlockSpec(memory_space=pltpu.SMEM),
        ],
        out_specs=[
            pl.BlockSpec((3, cells_x, 8, cells_z), lambda i: (0, 0, i, 0)),
            pl.BlockSpec((1, 8, 256), lambda i: (i, 0, 0)),
        ],
        out_shape=[
            jax.ShapeDtypeStruct((3, cells_x, rows_y, cells_z), F32),
            jax.ShapeDtypeStruct((rows_y // 8, 8, 256), F32),
        ],
        scratch_shapes=[pltpu.VMEM((256, 768), F32)],
        compiler_params=pltpu.CompilerParams(vmem_limit_bytes=24 << 20),
        name="back",
    )(mid, incoming, dep, band_depth, band_mix.reshape(-1))


def scan_x(total):
    count = lax.axis_size("gx")
    pieces = total.reshape(count, -1, total.shape[-1])
    pieces = lax.all_to_all(pieces, "gx", 0, 0, tiled=True)
    pieces = jnp.cumsum(pieces, axis=0) - pieces
    pieces = lax.all_to_all(pieces, "gx", 0, 0, tiled=True)
    return pieces.reshape(total.shape)


def composite(parts, cells_x):
    ndev = lax.axis_size("gz")
    me = lax.axis_index("gz")
    slabs = parts.shape[0]
    parts = parts.reshape(ndev, slabs // ndev, 8, parts.shape[-1])
    held = []
    for apart in range(ndev):
        piece = lax.dynamic_index_in_dim(parts, (me + apart) % ndev, 0, keepdims=False)[:, :4]
        if apart:
            piece = lax.ppermute(piece, "gz", [(i, (i + apart) % ndev) for i in range(ndev)])
        held.append((piece, (me - apart) % ndev))
    colour = 0.0
    depth = 0.0
    for piece, source in held:
        ahead = 0.0
        for other, origin in held:
            if other is not piece:
                ahead = ahead + jnp.where(origin < source, other[:, 3:], 0.0)
        colour = colour + jnp.exp(-ahead) * piece[:, :3]
        depth = depth + piece[:, 3:]
    image = jnp.concatenate([colour, 1.0 - jnp.exp(-depth)], axis=1)
    image = image.reshape(slabs // ndev, 4, cells_x, 8)
    return image.transpose(1, 2, 0, 3).reshape(4, cells_x, slabs // ndev * 8)


def body(features, w_in, b_in, w_out, b_out, band_depth, band_mix):
    cells_x = features.shape[1]
    total_x = cells_x * lax.axis_size("gx")
    total_z = features.shape[3] * lax.axis_size("gz")
    mid, total, dep = front(features, w_in, b_in, w_out, b_out, band_depth, total_x, total_z)
    incoming = scan_x(total)
    light, parts = back(mid, incoming, dep, band_depth, band_mix, total_x)
    return light, composite(parts, cells_x)


def solution(mesh):
    in_specs = (P(None, "gx", None, "gz"), P(), P(), P(), P(), P(), P())
    out_specs = (P(None, "gx", None, "gz"), P(None, "gx", "gz"))
    return jax.shard_map(body, mesh=mesh, in_specs=in_specs, out_specs=out_specs, check_vma=False)
```

time: 611 us -> 161 us (0.26)
  the two profiles are of different devices: /device:TPU:16 before, /device:TPU:0 now
where the time goes in v1:
time: 161 us
  Pallas kernels  94.3 us (59%)
  local copies, waits for them, and re-layouts  21 us (13%)
  blocking collectives  19 us (12%)
  waiting for transfers between devices  15.6 us (10%)
  starting transfers between devices  9.25 us (6%)
    pallas_call x1, Pallas kernels, front(): pl.pallas_call(functools.partial(front_kernel, total_x, total_z, 2), grid...  79.4 us
    unnamed x20, local copies, waits for them, and re-layouts  20.7 us
    all_to_all x1, blocking collectives, scan_x(): pieces = lax.all_to_all(pieces, 'gx', 0, 0, tiled=True)  19 us
    pallas_call x1, Pallas kernels, back(): pl.pallas_call(functools.partial(back_kernel, total_x, 4), grid=(rows_y /...  14.9 us
    all_to_all x1, waiting for transfers between devices, scan_x(): pieces = lax.all_to_all(pieces, 'gx', 0, 0, tiled=True)  11.6 us
    ppermute x3, starting transfers between devices, composite(): lax.ppermute(piece, 'gz', [(i, (i + apart) % ndev) for i in range(ndev)])  5.36 us
    ppermute x3, waiting for transfers between devices, composite(): lax.ppermute(piece, 'gz', [(i, (i + apart) % ndev) for i in range(ndev)])  3.98 us
    all_to_all x1, starting transfers between devices, scan_x(): pieces = lax.all_to_all(pieces, 'gx', 0, 0, tiled=True)  3.89 us
  transfers between devices with their start and end apart: 4, of which 3 were waited for; matrix products, arithmetic and copies ran while one was open for 0% of the time, Pallas kernels for 0%

profile of v1, /device:TPU:0, one launch (start us, length us, event | category | flops | bytes accessed | tf_op | source)
XLA Modules:
  0.0 160.9 jit_solution(12316635020279832271)
XLA Ops:
  0.6 0.0 copy-start.4
  0.7 0.8 copy.10.win_ref
  1.4 0.7 copy-done.2
  2.1 0.7 copy-done.3
  2.8 0.7 copy-done.5
  3.4 0.7 copy-done.6
  4.1 79.4 %front.1 = (f32[12,32,128,128]{3,2,1,0:T(8,128)S(1)}, f32[8,128,128]{2,1,0:T(8,128)S(1)}, f32[16,8,256]{2,1,0:T(8,128)S(1)}) custom-call(f32[4,32,128,128]{3,2,1,0:T(8,128)} %f_ref.1, f32[16,4]{1,0:T(8,128)S(1)} %copy.10.win_ref, f32[1,16]{1,0:T(1,128)S(1)} %bitcast.27, f32[12,16]{1,0:T(8,128)S(1)} %copy-done.2, f32[1,12]{1,0:T(1,128)S(1)} %bitcast.28, ...), custom_call_target="tpu_custom_call" | custom-call | tf_op jit(solution)/shard_map/front/pallas_call | solution.py:180
  83.5 8.3 %copy-done = f32[12,32,128,128]{3,2,1,0:T(8,128)} copy-done((f32[12,32,128,128]{3,2,1,0:T(8,128)}, f32[12,32,128,128]{3,2,1,0:T(8,128)S(1)}, u32[]{:S(2)}) %copy-start) | copy-done | bytes 25165848
  91.8 19.0 %all_to_all.10 = f32[32,32,128]{2,1,0:T(8,128)S(1)} all-to-all(f32[32,32,128]{2,1,0:T(8,128)S(1)} %bitcast.25), channel_id=1, replica_groups=mesh['gx'=32,'gz'=4] {'gx'}, dimensions={0} | all-to-all | bytes 1048576 | tf_op jit(solution)/shard_map/all_to_all | solution.py:238
  110.8 0.8 reduce-window_subtract_fusion
  111.6 3.9 %all-to-all-start.1 = ((f32[32,32,128]{2,1,0:T(8,128)}), f32[32,32,128]{2,1,0:T(8,128)S(1)}, u32[]{:S(2)}, u32[]{:S(2)}) async-start(f32[32,32,128]{2,1,0:T(8,128)} %reduce-window_subtract_fusion), calls=%async_computation.1 | async-start | bytes 1048576 | tf_op jit(solution)/shard_map/all_to_all | solution.py:240
  115.6 0.1 reshape.24.mix_ref
  115.7 11.6 %all-to-all-done.1 = f32[32,32,128]{2,1,0:T(8,128)S(1)} async-done(((f32[32,32,128]{2,1,0:T(8,128)}), f32[32,32,128]{2,1,0:T(8,128)S(1)}, u32[]{:S(2)}, u32[]{:S(2)}) %all-to-all-start.1) | async-done | bytes 524320 | tf_op jit(solution)/shard_map/all_to_all | solution.py:240
  127.3 8.2 %copy-done.1 = f32[12,32,128,128]{3,2,1,0:T(8,128)S(1)} copy-done((f32[12,32,128,128]{3,2,1,0:T(8,128)S(1)}, f32[12,32,128,128]{3,2,1,0:T(8,128)}, u32[]{:S(2)}) %copy-start.1) | copy-done | bytes 25165848
  135.5 14.9 %back.1 = (f32[3,32,128,128]{3,2,1,0:T(8,128)}, f32[16,8,256]{2,1,0:T(8,128)S(1)}) custom-call(f32[12,32,128,128]{3,2,1,0:T(8,128)S(1)} %copy-done.1, f32[8,128,128]{2,1,0:T(8,128)S(1)} %bitcast.24, f32[16,8,256]{2,1,0:T(8,128)S(1)} %get-tuple-element.9.dep_ref, f32[8]{0:T(128)S(1)} %copy-done.4, f32[24]{0:T(128)S(1)} %reshape.24.mix_ref), custom_call_target="tpu_custom_call" | custom-call | tf_op jit(solution)/shard_map/back/pallas_call | solution.py:211
  150.4 4.1 %collective-permute-start.2 = (f32[4,4,256]{2,1,0:T(4,128)S(1)}, f32[4,4,256]{2,1,0:T(4,128)S(1)}, u32[]{:S(2)}, u32[]{:S(2)}) collective-permute-start(f32[4,4,256]{2,1,0:T(4,128)S(1)} %slice.63), channel_id=1, source_target_pairs={{0,3},{1,0},{2,1},{3,2},{4,7},{5,4},{6,5},{7,6},{8,11},{9,8},{10,9... | collective-permute-start | bytes 49160 | tf_op jit(solution)/shard_map/ppermute | solution.py:253
  154.5 0.0 collective-permute-start.1
  154.5 1.3 collective-permute-start
  155.8 0.2 collective-permute-done.2
  156.0 3.8 %collective-permute-done.1 = f32[4,4,256]{2,1,0:T(4,128)S(1)} collective-permute-done((f32[4,4,256]{2,1,0:T(4,128)S(1)}, f32[4,4,256]{2,1,0:T(4,128)S(1)}, u32[]{:S(2)}, u32[]{:S(2)}) %collective-permute-start.1) | collective-permute-done | bytes 16416 | tf_op jit(solution)/shard_map/ppermute | solution.py:253
  159.8 0.0 collective-permute-done
  159.9 0.2 reshape.26
  160.1 0.1 copy.11
  160.2 0.7 copy.12
  (19 shorter events, 0.2 us)
Async XLA Ops:
  0.6 126.7 %copy-start.4 = (f32[8]{0:T(128)S(1)}, f32[8]{0:T(128)}, u32[]{:S(2)}) copy-start(f32[8]{0:T(128)} %depth_ref.3) | copy-start | bytes 100
  0.6 114.9 %copy-start.7 = (f32[3,8]{1,0:T(4,128)S(1)}, f32[3,8]{1,0:T(4,128)}, u32[]{:S(2)}) copy-start(f32[3,8]{1,0:T(4,128)} %param.13) | copy-start | bytes 292
  1.4 0.7 copy-start.2
  2.1 0.7 copy-start.3
  2.8 0.7 copy-start.5
  3.4 0.7 copy-start.6
  83.5 8.3 %copy-start = (f32[12,32,128,128]{3,2,1,0:T(8,128)}, f32[12,32,128,128]{3,2,1,0:T(8,128)S(1)}, u32[]{:S(2)}) copy-start(f32[12,32,128,128]{3,2,1,0:T(8,128)S(1)} %get-tuple-element.7.mid_ref) | copy-start | bytes 75497472
  111.6 15.7 %all-to-all-start.1 = ((f32[32,32,128]{2,1,0:T(8,128)}), f32[32,32,128]{2,1,0:T(8,128)S(1)}, u32[]{:S(2)}, u32[]{:S(2)}) async-start(f32[32,32,128]{2,1,0:T(8,128)} %reduce-window_subtract_fusion), calls=%async_computation.1 | async-start | bytes 1048576 | tf_op jit(solution)/shard_map/all_to_all | solution.py:240
  127.3 8.2 %copy-start.1 = (f32[12,32,128,128]{3,2,1,0:T(8,128)S(1)}, f32[12,32,128,128]{3,2,1,0:T(8,128)}, u32[]{:S(2)}) copy-start(f32[12,32,128,128]{3,2,1,0:T(8,128)} %copy-done) | copy-start | bytes 75497472
  150.4 5.5 %collective-permute-start.2 = (f32[4,4,256]{2,1,0:T(4,128)S(1)}, f32[4,4,256]{2,1,0:T(4,128)S(1)}, u32[]{:S(2)}, u32[]{:S(2)}) collective-permute-start(f32[4,4,256]{2,1,0:T(4,128)S(1)} %slice.63), channel_id=1, source_target_pairs={{0,3},{1,0},{2,1},{3,2},{4,7},{5,4},{6,5},{7,6},{8,11},{9,8},{10,9... | collective-permute-start | bytes 49160 | tf_op jit(solution)/shard_map/ppermute | solution.py:253
  154.5 5.2 %collective-permute-start.1 = (f32[4,4,256]{2,1,0:T(4,128)S(1)}, f32[4,4,256]{2,1,0:T(4,128)S(1)}, u32[]{:S(2)}, u32[]{:S(2)}) collective-permute-start(f32[4,4,256]{2,1,0:T(4,128)S(1)} %slice.61), channel_id=1, source_target_pairs={{0,2},{1,3},{2,0},{3,1},{4,6},{5,7},{6,4},{7,5},{8,10},{9,11},{10,... | collective-permute-start | bytes 49160 | tf_op jit(solution)/shard_map/ppermute | solution.py:253
  154.5 5.2 %collective-permute-start = (f32[4,4,256]{2,1,0:T(4,128)S(1)}, f32[4,4,256]{2,1,0:T(4,128)S(1)}, u32[]{:S(2)}, u32[]{:S(2)}) collective-permute-start(f32[4,4,256]{2,1,0:T(4,128)S(1)} %slice.59), channel_id=1, source_target_pairs={{0,1},{1,2},{2,3},{3,0},{4,5},{5,6},{6,7},{7,4},{8,9},{9,10},{10,1... | collective-permute-start | bytes 49160 | tf_op jit(solution)/shard_map/ppermute | solution.py:253

commit v2 on v1

v2 whole, which is shorter than its diff:
```python
import functools
import math

import jax
import jax.numpy as jnp
from jax import lax
from jax.experimental import pallas as pl
from jax.experimental.pallas import tpu as pltpu
from jax.sharding import PartitionSpec as P

BANDS = 8
UNITS = 16
FEATS = 4
OUTS = 12
SLAB = 16
CHUNKS = 1
LOG2E = math.log2(math.e)
F32 = jnp.float32
BF16 = jnp.bfloat16


def iota(shape, dim):
    return lax.broadcasted_iota(jnp.int32, shape, dim)


def split(value):
    high = value.astype(BF16)
    return high, (value - high.astype(F32)).astype(BF16)


def exact_dot(a, b):
    return jnp.dot(a, b, precision=lax.Precision.HIGHEST, preferred_element_type=F32)


def one_hot(shape, condition):
    return jnp.where(condition, jnp.ones(shape, F32), jnp.zeros(shape, F32))


def bias_columns(column):
    rows = column.shape[0]
    high = column.astype(BF16).astype(F32)
    rest = column - high
    middle = rest.astype(BF16).astype(F32)
    low = rest - middle
    lane = iota((rows, 16), 1)
    zero = jnp.zeros((rows, 16), F32)
    return jnp.where(
        lane == 0, high, jnp.where(lane == 1, middle, jnp.where(lane == 2, low, zero))
    ).astype(BF16)


def build_first(w_in, b_in):
    rows, cols = SLAB * UNITS, FEATS * SLAB
    pick = one_hot((rows, UNITS), iota((rows, UNITS), 0) % UNITS == iota((rows, UNITS), 1))
    spread = one_hot((FEATS, cols), iota((FEATS, cols), 1) // SLAB == iota((FEATS, cols), 0))
    full = exact_dot(exact_dot(pick, w_in), spread)
    full = jnp.where(iota((rows, cols), 0) // UNITS == iota((rows, cols), 1) % SLAB, full, 0.0)
    high, low = split(full)
    bias = bias_columns(jnp.sum(pick * b_in, axis=1, keepdims=True))
    return high, low, bias


def build_second(w_out, b_out):
    rows, cols = OUTS * 8, 8 * UNITS
    pick = one_hot((rows, OUTS), iota((rows, OUTS), 0) // 8 == iota((rows, OUTS), 1))
    spread = one_hot((UNITS, cols), iota((UNITS, cols), 1) % UNITS == iota((UNITS, cols), 0))
    full = exact_dot(exact_dot(pick, w_out), spread)
    full = jnp.where(iota((rows, cols), 0) % 8 == iota((rows, cols), 1) // UNITS, full, 0.0)
    out = iota((rows, 1), 0) // 8
    scale = jnp.where((out >= BANDS) & (out < BANDS + 3), -LOG2E, 1.0)
    high, low = split(full * scale)
    bias = bias_columns(jnp.sum(pick * b_out, axis=1, keepdims=True) * scale)
    return high, low, bias


def softplus(x):
    return jnp.maximum(jnp.log(1.0 + jnp.exp(jnp.minimum(x, 80.0))), x)


def front_kernel(total_x, total_z, batch, unroll, f_ref, win_ref, bin_ref, wout_ref, bout_ref, depth_ref,
                 mid_ref, sum_ref, dep_ref, first_ref, second_ref, tri_ref):
    cells_x = f_ref.shape[1]
    step = pl.program_id(0)

    @pl.when(step == 0)
    def _():
        high, low, bias = build_first(win_ref[...].T, bin_ref[...])
        first_ref[:, 0:64] = high
        first_ref[:, 64:128] = high
        first_ref[:, 128:192] = low
        first_ref[:, 192:208] = bias
        high, low, bias = build_second(wout_ref[...], bout_ref[...])
        second_ref[:, 0:128] = high
        second_ref[:, 128:256] = high
        second_ref[:, 256:384] = low
        second_ref[:, 384:400] = bias
        tri_ref[...] = one_hot((256, 128), iota((256, 128), 0) % 128 < iota((256, 128), 1)).astype(BF16)

    ones = jnp.ones((16, 128 * batch), BF16)
    rates = [depth_ref[b] * (-LOG2E / total_x) for b in range(BANDS)]
    fade = -LOG2E / total_z

    def layer_one(x0):
        rows = jnp.concatenate(
            [jnp.concatenate([f_ref[c, x0 + s] for s in range(batch)], axis=1) for c in range(FEATS)], axis=0
        )
        high, low = split(rows)
        return jnp.dot(first_ref[...], jnp.concatenate([high, low, high, ones], axis=0),
                       preferred_element_type=F32)

    def layer_two(hidden):
        high, low = split(jnp.maximum(hidden, 0.0))
        raws = []
        for j in range(2):
            part = slice(j * 128, j * 128 + 128)
            raws.append(jnp.dot(second_ref[...],
                                jnp.concatenate([high[part], low[part], high[part], ones], axis=0),
                                preferred_element_type=F32))
        return raws

    def finish(x0, raws, sums):
        sums = list(sums)
        for j in range(2):
            here = slice(8 * j, 8 * j + 8)
            for s in range(batch):
                x = x0 + s
                tile = raws[j][:, s * 128 : s * 128 + 128]
                for b in range(BANDS):
                    total = sums[j * BANDS + b]
                    mid_ref[0, b, x, here, :] = jnp.exp2(total * rates[b])
                    sums[j * BANDS + b] = total + softplus(tile[8 * b : 8 * b + 8])
                for k in range(BANDS, BANDS + 3):
                    mid_ref[0, k, x, here, :] = pl.reciprocal(
                        1.0 + jnp.exp2(tile[8 * k : 8 * k + 8]), approx=True)
                mid_ref[0, BANDS + 3, x, here, :] = softplus(tile[8 * BANDS + 24 : 8 * BANDS + 32])
        return tuple(sums)

    zero = jnp.zeros((8, 128), F32)
    sums = (zero,) * (2 * BANDS)
    count = cells_x // batch
    hidden, raws = {}, {}
    for t in range(count + unroll):
        if t < count:
            hidden[t] = layer_one(t * batch)
        if unroll == 2 and 1 <= t <= count:
            raws[t - 1] = layer_two(hidden.pop(t - 1))
        if t >= unroll:
            if unroll == 1:
                raws[t - 1] = layer_two(hidden.pop(t - 1))
            sums = finish((t - unroll) * batch, raws.pop(t - unroll), sums)
    select = one_hot((8, 256), iota((8, 256), 0) == 3).astype(BF16)
    for j in range(2):
        for b in range(BANDS):
            sum_ref[b, 8 * j : 8 * j + 8, :] = sums[j * BANDS + b]
        here = slice(8 * j, 8 * j + 8)
        kappa = mid_ref[0, BANDS + 3, :, here, :].reshape(8 * cells_x, 128)
        both = jnp.concatenate(split(kappa), axis=1)
        occlusion = jnp.dot(both, tri_ref[...], preferred_element_type=F32)
        weight = jnp.exp2(occlusion * fade) * (1.0 - jnp.exp2(kappa * fade))
        mid_ref[0, BANDS + 3, :, here, :] = weight.reshape(cells_x, 8, 128)
        dep_ref[j] = lax.dot_general(select, both, (((1,), (1,)), ((), ())),
                                     preferred_element_type=F32) * (1.0 / total_z)


def back_kernel(total_x, unroll, mid_ref, inc_ref, dep_ref, depth_ref, mix_ref,
                light_ref, img_ref, prod_ref):
    cells_x = light_ref.shape[1]
    select = one_hot((8, 768), iota((8, 768), 0) == iota((8, 768), 1) // 256).astype(BF16)
    for j in range(2):
        here = slice(8 * j, 8 * j + 8)
        gains = []
        for b in range(BANDS):
            fade = jnp.exp2(inc_ref[b, here] * (depth_ref[b] * (-LOG2E / total_x)))
            gains.append([fade * mix_ref[k, b] for k in range(3)])

        def two(i, carry):
            products = [[], [], []]
            for x in (2 * i, 2 * i + 1):
                bands = [mid_ref[0, b, x, here, :] for b in range(BANDS)]
                weight = mid_ref[0, BANDS + 3, x, here, :]
                for k in range(3):
                    total = bands[0] * gains[0][k]
                    for b in range(1, BANDS):
                        total = total + bands[b] * gains[b][k]
                    light = total * mid_ref[0, BANDS + k, x, here, :]
                    light_ref[k, x, here, :] = light
                    products[k].append(light * weight)
            rows = pl.ds(pl.multiple_of(i * 16, 16), 16)
            for k in range(3):
                high, low = split(jnp.concatenate(products[k], axis=0))
                prod_ref[rows, 256 * k : 256 * k + 128] = high
                prod_ref[rows, 256 * k + 128 : 256 * k + 256] = low
            return carry

        lax.fori_loop(0, cells_x // 2, two, 0, unroll=unroll)
        img_ref[j] = lax.dot_general(select, prod_ref[...], (((1,), (1,)), ((), ())),
                                     preferred_element_type=F32) + dep_ref[j]


def front(features, w_in, b_in, w_out, b_out, band_depth, total_x, total_z, first, rows_y):
    _, cells_x, _, cells_z = features.shape
    skip = first // SLAB

    def small(*shape):
        return pl.BlockSpec(shape, lambda i: (0,) * len(shape))

    return pl.pallas_call(
        functools.partial(front_kernel, total_x, total_z, 4, 1),
        grid=(rows_y // SLAB,),
        in_specs=[
            pl.BlockSpec((FEATS, cells_x, SLAB, cells_z), lambda i: (0, 0, i + skip, 0)),
            small(FEATS, UNITS), small(1, UNITS), small(OUTS, UNITS), small(1, OUTS),
            pl.BlockSpec(memory_space=pltpu.SMEM),
        ],
        out_specs=[
            pl.BlockSpec((1, OUTS, cells_x, SLAB, cells_z), lambda i: (i, 0, 0, 0, 0)),
            pl.BlockSpec((BANDS, SLAB, cells_z), lambda i: (0, i, 0)),
            pl.BlockSpec((2, 8, 256), lambda i: (i, 0, 0)),
        ],
        out_shape=[
            jax.ShapeDtypeStruct((rows_y // SLAB, OUTS, cells_x, SLAB, cells_z), F32),
            jax.ShapeDtypeStruct((BANDS, rows_y, cells_z), F32),
            jax.ShapeDtypeStruct((rows_y // 8, 8, 256), F32),
        ],
        scratch_shapes=[
            pltpu.VMEM((SLAB * UNITS, 208), BF16),
            pltpu.VMEM((OUTS * 8, 400), BF16),
            pltpu.VMEM((256, 128), BF16),
        ],
        compiler_params=pltpu.CompilerParams(vmem_limit_bytes=30 << 20),
        name="front",
    )(*(pltpu.with_memory_space_constraint(value, pltpu.HBM)
        for value in (features, w_in.T, b_in[None], w_out, b_out[None])), band_depth)


def back(mid, incoming, dep, band_depth, band_mix, light, total_x, first, whole_y):
    slabs, _, cells_x, _, cells_z = mid.shape
    skip = first // SLAB
    operands = [mid, incoming, dep, band_depth, band_mix]
    in_specs = [
        pl.BlockSpec((1, OUTS, cells_x, SLAB, cells_z), lambda i: (i, 0, 0, 0, 0)),
        pl.BlockSpec((BANDS, SLAB, cells_z), lambda i: (0, i, 0)),
        pl.BlockSpec((2, 8, 256), lambda i: (i, 0, 0)),
        pl.BlockSpec(memory_space=pltpu.SMEM),
        pl.BlockSpec(memory_space=pltpu.SMEM),
    ]
    kernel = functools.partial(back_kernel, total_x, 4)
    aliases = {}
    if light is not None:
        operands.append(light)
        in_specs.append(pl.BlockSpec(memory_space=pl.ANY))
        aliases = {len(operands) - 1: 0}
        inner = kernel

        def kernel(*refs):
            inner(*refs[:5], *refs[6:])

    return pl.pallas_call(
        kernel,
        grid=(slabs,),
        in_specs=in_specs,
        out_specs=[
            pl.BlockSpec((3, cells_x, SLAB, cells_z), lambda i: (0, 0, i + skip, 0)),
            pl.BlockSpec((2, 8, 256), lambda i: (i, 0, 0)),
        ],
        out_shape=[
            jax.ShapeDtypeStruct((3, cells_x, whole_y, cells_z), F32),
            jax.ShapeDtypeStruct((2 * slabs, 8, 256), F32),
        ],
        scratch_shapes=[pltpu.VMEM((256, 768), BF16)],
        input_output_aliases=aliases,
        compiler_params=pltpu.CompilerParams(vmem_limit_bytes=30 << 20),
        name="back",
    )(*operands)


def swap(value, axis, partner):
    return lax.ppermute(value, axis, [(i, partner(i)) for i in range(lax.axis_size(axis))])


def across(i, bit):
    return i ^ 1 if bit == 0 else 3 - i


def scan_x(total):
    half = BANDS // 2
    me = lax.axis_index("gx")
    core, place = me % 2, (me // 2 % 4, me // 8)
    low, high = total[:half], total[half:]
    keep = jnp.where(core == 0, low, high)
    got = swap(jnp.where(core == 0, high, low), "gx", lambda i: i ^ 1)
    total = keep + got
    before = jnp.zeros_like(total)
    for axis in range(2):
        for bit in range(2):
            def partner(i):
                if axis == 0:
                    return i // 8 * 8 + across(i // 2 % 4, bit) * 2 + i % 2
                return across(i // 8, bit) * 8 + i % 8
            other = swap(total, "gx", partner)
            before = before + jnp.where(place[axis] >> bit & 1, other, 0.0)
            total = total + other
    mine = before + jnp.where(core == 0, 0.0, got)
    theirs = swap(before + jnp.where(core == 0, keep, 0.0), "gx", lambda i: i ^ 1)
    return jnp.concatenate([jnp.where(core == 0, mine, theirs), jnp.where(core == 0, theirs, mine)], axis=0)


def composite(parts, cells_x):
    ndev = lax.axis_size("gz")
    me = lax.axis_index("gz")
    slabs = parts.shape[0]
    parts = parts.reshape(ndev, slabs // ndev, 8, parts.shape[-1])
    held = []
    for apart in range(ndev):
        piece = lax.dynamic_index_in_dim(parts, (me + apart) % ndev, 0, keepdims=False)[:, :4]
        if apart:
            piece = lax.ppermute(piece, "gz", [(i, (i + apart) % ndev) for i in range(ndev)])
        held.append((piece, (me - apart) % ndev))
    colour = 0.0
    depth = 0.0
    for piece, source in held:
        ahead = 0.0
        for other, origin in held:
            if other is not piece:
                ahead = ahead + jnp.where(origin < source, other[:, 3:], 0.0)
        colour = colour + jnp.exp(-ahead) * piece[:, :3]
        depth = depth + piece[:, 3:]
    image = jnp.concatenate([colour, 1.0 - jnp.exp(-depth)], axis=1)
    image = image.reshape(slabs // ndev, 4, cells_x, 8)
    return image.transpose(1, 2, 0, 3).reshape(4, cells_x, slabs // ndev * 8)


def body(features, w_in, b_in, w_out, b_out, band_depth, band_mix):
    cells_x = features.shape[1]
    total_x = cells_x * lax.axis_size("gx")
    total_z = features.shape[3] * lax.axis_size("gz")
    rows_y = features.shape[2]
    size = rows_y // CHUNKS
    pieces = [
        front(features, w_in, b_in, w_out, b_out, band_depth, total_x, total_z, c * size, size)
        for c in range(CHUNKS)
    ]
    incoming = [scan_x(piece[1]) for piece in pieces]
    light, parts = None, []
    for c, (mid, _, dep) in enumerate(pieces):
        light, part = back(mid, incoming[c], dep, band_depth, band_mix, light, total_x, c * size, rows_y)
        parts.append(part)
    parts = jnp.concatenate(parts, axis=0)
    return light, composite(parts, cells_x)


def solution(mesh):
    in_specs = (P(None, "gx", None, "gz"), P(), P(), P(), P(), P(), P())
    out_specs = (P(None, "gx", None, "gz"), P(None, "gx", "gz"))
    return jax.shard_map(body, mesh=mesh, in_specs=in_specs, out_specs=out_specs, check_vma=False)
```

time: 161 us -> 86 us (0.53)
  Pallas kernels: 94.3 us -> 38.5 us
  local copies, waits for them, and re-layouts: 21 us -> 1.69 us
  blocking collectives: 19 us -> 0 us
  waiting for transfers between devices: 15.6 us -> 27.8 us
  starting transfers between devices: 9.25 us -> 16.3 us
    pallas_call x2, Pallas kernels: 94.3 us -> 38.5 us  [the longest x1 22.3 us: front(): pl.pallas_call(functools.partial(front_kernel, total_x, total_z, 4, 1), g...]
    ppermute x0 -> x6, waiting for transfers between devices: none -> 25.1 us  [swap(): lax.ppermute(value, axis, [(i, partner(i)) for i in range(lax.axis_size(a...]
    unnamed x20 -> x9, local copies, waits for them, and re-layouts: 20.7 us -> 1.39 us
    all_to_all x1 -> x0, blocking collectives: 19 us -> none  [scan_x(): pieces = lax.all_to_all(pieces, 'gx', 0, 0, tiled=True)]
    all_to_all x1 -> x0, waiting for transfers between devices: 11.6 us -> none  [scan_x(): pieces = lax.all_to_all(pieces, 'gx', 0, 0, tiled=True)]
    ppermute x0 -> x6, starting transfers between devices: none -> 9.65 us  [swap(): lax.ppermute(value, axis, [(i, partner(i)) for i in range(lax.axis_size(a...]
    all_to_all x1 -> x0, starting transfers between devices: 3.89 us -> none  [scan_x(): pieces = lax.all_to_all(pieces, 'gx', 0, 0, tiled=True)]
  transfers between devices with their start and end apart: 4 -> 9, of which waited for: 3 -> 8; matrix products, arithmetic and copies ran while one was open for 0% -> 0% of each run, Pallas kernels for 0% -> 0%
where the time goes in v2:
time: 86 us; the launch traced here: 85.7 us
  Pallas kernels  38.5 us (45%)
  waiting for transfers between devices  27.8 us (32%)
  starting transfers between devices  16.3 us (19%)
  local copies, waits for them, and re-layouts  1.69 us (2%)
    ppermute x6, waiting for transfers between devices, swap(): lax.ppermute(value, axis, [(i, partner(i)) for i in range(lax.axis_size(a...  25.1 us
    pallas_call x1, Pallas kernels, front(): pl.pallas_call(functools.partial(front_kernel, total_x, total_z, 4, 1), g...  22.3 us
    pallas_call x1, Pallas kernels, back(): pl.pallas_call(kernel, grid=(slabs,), in_specs=in_specs, out_specs=[pl.Bl...  16.2 us
    ppermute x6, starting transfers between devices, swap(): lax.ppermute(value, axis, [(i, partner(i)) for i in range(lax.axis_size(a...  9.65 us
    ppermute x3, starting transfers between devices, composite(): lax.ppermute(piece, 'gz', [(i, (i + apart) % ndev) for i in range(ndev)])  6.66 us
    ppermute x3, waiting for transfers between devices, composite(): lax.ppermute(piece, 'gz', [(i, (i + apart) % ndev) for i in range(ndev)])  2.73 us
  transfers between devices with their start and end apart: 9, of which 8 were waited for; matrix products, arithmetic and copies ran while one was open for 0% of the time, Pallas kernels for 0%

profile of v2, /device:TPU:0, one launch (start us, length us, event | category | flops | bytes accessed | tf_op | source)
XLA Modules:
  0.0 85.7 jit_solution(15323559521353926152)
XLA Ops:
  0.7 0.6 copy-done.1
  1.3 22.3 %front.1 = (f32[8,12,32,16,128]{4,3,2,1,0:T(8,128)}, f32[8,128,128]{2,1,0:T(8,128)S(1)}, f32[16,8,256]{2,1,0:T(8,128)S(1)}) custom-call(f32[4,32,128,128]{3,2,1,0:T(8,128)} %f_ref.1, f32[4,16]{1,0:T(4,128)} %bitcast.25, f32[1,16]{1,0:T(1,128)} %bitcast.26, f32[12,16]{1,0:T(8,128)} %wout_ref.1, f32[1,12]{1,0:T(1,128)} %bitcast.27, f32[8]{0:T(128)S(1)} %copy-done.1), custom_call_target="tpu_custom_call" | custom-call | tf_op jit(solution)/shard_map/front/pallas_call | solution.py:207
  23.6 0.1 collective-permute-start
  23.7 1.5 %collective-permute-done = f32[4,128,128]{2,1,0:T(8,128)S(1)} collective-permute-done((f32[4,128,128]{2,1,0:T(8,128)S(1)}, f32[4,128,128]{2,1,0:T(8,128)S(1)}, u32[]{:S(2)}, u32[]{:S(2)}) %collective-permute-start) | collective-permute-done | bytes 262176 | tf_op jit(solution)/shard_map/ppermute | solution.py:278
  25.3 1.7 %collective-permute-start.1 = (f32[4,128,128]{2,1,0:T(8,128)S(1)}, f32[4,128,128]{2,1,0:T(8,128)S(1)}, u32[]{:S(2)}, u32[]{:S(2)}) collective-permute-start(f32[4,128,128]{2,1,0:T(8,128)S(1)} %fusion), channel_id=1, source_target_pairs={{0,8},{4,12},{8,0},{12,4},{16,24},{20,28},{24,16},{28,20},{32,40},... | collective-permute-start | bytes 786440 | tf_op jit(solution)/shard_map/ppermute | solution.py:278
  27.0 6.8 %collective-permute-done.1 = f32[4,128,128]{2,1,0:T(8,128)S(1)} collective-permute-done((f32[4,128,128]{2,1,0:T(8,128)S(1)}, f32[4,128,128]{2,1,0:T(8,128)S(1)}, u32[]{:S(2)}, u32[]{:S(2)}) %collective-permute-start.1) | collective-permute-done | bytes 262176 | tf_op jit(solution)/shard_map/ppermute | solution.py:278
  33.8 2.9 %collective-permute-start.2 = (f32[4,128,128]{2,1,0:T(8,128)S(1)}, f32[4,128,128]{2,1,0:T(8,128)S(1)}, u32[]{:S(2)}, u32[]{:S(2)}) collective-permute-start(f32[4,128,128]{2,1,0:T(8,128)S(1)} %add.128), channel_id=1, source_target_pairs={{0,24},{4,28},{8,16},{12,20},{16,8},{20,12},{24,0},{28,4},{32,56},... | collective-permute-start | bytes 786440 | tf_op jit(solution)/shard_map/ppermute | solution.py:278
  36.7 5.9 %collective-permute-done.2 = f32[4,128,128]{2,1,0:T(8,128)S(1)} collective-permute-done((f32[4,128,128]{2,1,0:T(8,128)S(1)}, f32[4,128,128]{2,1,0:T(8,128)S(1)}, u32[]{:S(2)}, u32[]{:S(2)}) %collective-permute-start.2) | collective-permute-done | bytes 262176 | tf_op jit(solution)/shard_map/ppermute | solution.py:278
  42.6 1.7 %collective-permute-start.3 = (f32[4,128,128]{2,1,0:T(8,128)S(1)}, f32[4,128,128]{2,1,0:T(8,128)S(1)}, u32[]{:S(2)}, u32[]{:S(2)}) collective-permute-start(f32[4,128,128]{2,1,0:T(8,128)S(1)} %add.130), channel_id=1, source_target_pairs={{0,32},{4,36},{8,40},{12,44},{16,48},{20,52},{24,56},{28,60},{32,0... | collective-permute-start | bytes 786440 | tf_op jit(solution)/shard_map/ppermute | solution.py:278
  44.4 4.9 %collective-permute-done.3 = f32[4,128,128]{2,1,0:T(8,128)S(1)} collective-permute-done((f32[4,128,128]{2,1,0:T(8,128)S(1)}, f32[4,128,128]{2,1,0:T(8,128)S(1)}, u32[]{:S(2)}, u32[]{:S(2)}) %collective-permute-start.3) | collective-permute-done | bytes 262176 | tf_op jit(solution)/shard_map/ppermute | solution.py:278
  49.4 3.2 %collective-permute-start.4 = (f32[4,128,128]{2,1,0:T(8,128)S(1)}, f32[4,128,128]{2,1,0:T(8,128)S(1)}, u32[]{:S(2)}, u32[]{:S(2)}) collective-permute-start(f32[4,128,128]{2,1,0:T(8,128)S(1)} %add.132), channel_id=1, source_target_pairs={{0,96},{4,100},{8,104},{12,108},{16,112},{20,116},{24,120},{28,124... | collective-permute-start | bytes 786440 | tf_op jit(solution)/shard_map/ppermute | solution.py:278
  52.5 4.5 %collective-permute-done.4 = f32[4,128,128]{2,1,0:T(8,128)S(1)} collective-permute-done((f32[4,128,128]{2,1,0:T(8,128)S(1)}, f32[4,128,128]{2,1,0:T(8,128)S(1)}, u32[]{:S(2)}, u32[]{:S(2)}) %collective-permute-start.4) | collective-permute-done | bytes 262176 | tf_op jit(solution)/shard_map/ppermute | solution.py:278
  57.0 0.1 select_add_fusion
  57.1 0.1 collective-permute-start.5
  57.3 1.5 %collective-permute-done.5 = f32[4,128,128]{2,1,0:T(8,128)S(1)} collective-permute-done((f32[4,128,128]{2,1,0:T(8,128)S(1)}, f32[4,128,128]{2,1,0:T(8,128)S(1)}, u32[]{:S(2)}, u32[]{:S(2)}) %collective-permute-start.5) | collective-permute-done | bytes 262176 | tf_op jit(solution)/shard_map/ppermute | solution.py:278
  58.9 16.2 %back.1 = (f32[3,32,128,128]{3,2,1,0:T(8,128)}, f32[16,8,256]{2,1,0:T(8,128)S(1)}) custom-call(f32[8,12,32,16,128]{4,3,2,1,0:T(8,128)} %get-tuple-element.7.mid_ref, f32[8,128,128]{2,1,0:T(8,128)S(1)} %pad_maximum_fusion.inc_ref, f32[16,8,256]{2,1,0:T(8,128)S(1)} %get-tuple-element.9.dep_ref, f32[8]{0:T(128)S(1)} %copy-done.2, f32[3,8]{1,0:T(4,128)S(1)} %copy-done), custom_call_target="tpu_custom_call" | custom-call | tf_op jit(solution)/shard_map/back/pallas_call | solution.py:258
  75.1 2.1 %collective-permute-start.6 = (f32[4,4,256]{2,1,0:T(4,128)S(1)}, f32[4,4,256]{2,1,0:T(4,128)S(1)}, u32[]{:S(2)}, u32[]{:S(2)}) collective-permute-start(f32[4,4,256]{2,1,0:T(4,128)S(1)} %slice.67), channel_id=1, source_target_pairs={{0,1},{1,2},{2,3},{3,0},{4,5},{5,6},{6,7},{7,4},{8,9},{9,10},{10,1... | collective-permute-start | bytes 49160 | tf_op jit(solution)/shard_map/ppermute | solution.py:317
  77.2 3.6 %collective-permute-start.7 = (f32[4,4,256]{2,1,0:T(4,128)S(1)}, f32[4,4,256]{2,1,0:T(4,128)S(1)}, u32[]{:S(2)}, u32[]{:S(2)}) collective-permute-start(f32[4,4,256]{2,1,0:T(4,128)S(1)} %slice.69), channel_id=1, source_target_pairs={{0,2},{1,3},{2,0},{3,1},{4,6},{5,7},{6,4},{7,5},{8,10},{9,11},{10,... | collective-permute-start | bytes 49160 | tf_op jit(solution)/shard_map/ppermute | solution.py:317
  80.8 1.0 %collective-permute-start.8 = (f32[4,4,256]{2,1,0:T(4,128)S(1)}, f32[4,4,256]{2,1,0:T(4,128)S(1)}, u32[]{:S(2)}, u32[]{:S(2)}) collective-permute-start(f32[4,4,256]{2,1,0:T(4,128)S(1)} %slice.71), channel_id=1, source_target_pairs={{0,3},{1,0},{2,1},{3,2},{4,7},{5,4},{6,5},{7,6},{8,11},{9,8},{10,9... | collective-permute-start | bytes 49160 | tf_op jit(solution)/shard_map/ppermute | solution.py:317
  81.8 0.9 %collective-permute-done.7 = f32[4,4,256]{2,1,0:T(4,128)S(1)} collective-permute-done((f32[4,4,256]{2,1,0:T(4,128)S(1)}, f32[4,4,256]{2,1,0:T(4,128)S(1)}, u32[]{:S(2)}, u32[]{:S(2)}) %collective-permute-start.7) | collective-permute-done | bytes 16416 | tf_op jit(solution)/shard_map/ppermute | solution.py:317
  82.7 1.9 %collective-permute-done.8 = f32[4,4,256]{2,1,0:T(4,128)S(1)} collective-permute-done((f32[4,4,256]{2,1,0:T(4,128)S(1)}, f32[4,4,256]{2,1,0:T(4,128)S(1)}, u32[]{:S(2)}, u32[]{:S(2)}) %collective-permute-start.8) | collective-permute-done | bytes 16416 | tf_op jit(solution)/shard_map/ppermute | solution.py:317
  84.7 0.2 reshape.14
  84.9 0.1 copy.9
  85.0 0.7 copy.10
  (23 shorter events, 0.5 us)
Async XLA Ops:
  0.6 0.7 copy-start.1
  1.3 57.6 %copy-start = (f32[3,8]{1,0:T(4,128)S(1)}, f32[3,8]{1,0:T(4,128)}, u32[]{:S(2)}) copy-start(f32[3,8]{1,0:T(4,128)} %mix_ref.1) | copy-start | bytes 292
  1.3 57.6 %copy-start.2 = (f32[8]{0:T(128)S(1)}, f32[8]{0:T(128)}, u32[]{:S(2)}) copy-start(f32[8]{0:T(128)} %depth_ref.3) | copy-start | bytes 100
  23.6 1.6 %collective-permute-start = (f32[4,128,128]{2,1,0:T(8,128)S(1)}, f32[4,128,128]{2,1,0:T(8,128)S(1)}, u32[]{:S(2)}, u32[]{:S(2)}) collective-permute-start(f32[4,128,128]{2,1,0:T(8,128)S(1)} %slice_select_fusion), channel_id=1, source_target_pairs={{0,4},{4,0},{8,12},{12,8},{16,20},{20,16},{24,28},{28,24},{32,36},... | collective-permute-start | bytes 786440 | tf_op jit(solution)/shard_map/ppermute | solution.py:278
  25.3 8.4 %collective-permute-start.1 = (f32[4,128,128]{2,1,0:T(8,128)S(1)}, f32[4,128,128]{2,1,0:T(8,128)S(1)}, u32[]{:S(2)}, u32[]{:S(2)}) collective-permute-start(f32[4,128,128]{2,1,0:T(8,128)S(1)} %fusion), channel_id=1, source_target_pairs={{0,8},{4,12},{8,0},{12,4},{16,24},{20,28},{24,16},{28,20},{32,40},... | collective-permute-start | bytes 786440 | tf_op jit(solution)/shard_map/ppermute | solution.py:278
  33.8 8.8 %collective-permute-start.2 = (f32[4,128,128]{2,1,0:T(8,128)S(1)}, f32[4,128,128]{2,1,0:T(8,128)S(1)}, u32[]{:S(2)}, u32[]{:S(2)}) collective-permute-start(f32[4,128,128]{2,1,0:T(8,128)S(1)} %add.128), channel_id=1, source_target_pairs={{0,24},{4,28},{8,16},{12,20},{16,8},{20,12},{24,0},{28,4},{32,56},... | collective-permute-start | bytes 786440 | tf_op jit(solution)/shard_map/ppermute | solution.py:278
  42.6 6.7 %collective-permute-start.3 = (f32[4,128,128]{2,1,0:T(8,128)S(1)}, f32[4,128,128]{2,1,0:T(8,128)S(1)}, u32[]{:S(2)}, u32[]{:S(2)}) collective-permute-start(f32[4,128,128]{2,1,0:T(8,128)S(1)} %add.130), channel_id=1, source_target_pairs={{0,32},{4,36},{8,40},{12,44},{16,48},{20,52},{24,56},{28,60},{32,0... | collective-permute-start | bytes 786440 | tf_op jit(solution)/shard_map/ppermute | solution.py:278
  49.4 7.7 %collective-permute-start.4 = (f32[4,128,128]{2,1,0:T(8,128)S(1)}, f32[4,128,128]{2,1,0:T(8,128)S(1)}, u32[]{:S(2)}, u32[]{:S(2)}) collective-permute-start(f32[4,128,128]{2,1,0:T(8,128)S(1)} %add.132), channel_id=1, source_target_pairs={{0,96},{4,100},{8,104},{12,108},{16,112},{20,116},{24,120},{28,124... | collective-permute-start | bytes 786440 | tf_op jit(solution)/shard_map/ppermute | solution.py:278
  57.1 1.6 %collective-permute-start.5 = (f32[4,128,128]{2,1,0:T(8,128)S(1)}, f32[4,128,128]{2,1,0:T(8,128)S(1)}, u32[]{:S(2)}, u32[]{:S(2)}) collective-permute-start(f32[4,128,128]{2,1,0:T(8,128)S(1)} %get-tuple-element.14), channel_id=1, source_target_pairs={{0,4},{4,0},{8,12},{12,8},{16,20},{20,16},{24,28},{28,24},{32,36},... | collective-permute-start | bytes 786440 | tf_op jit(solution)/shard_map/ppermute | solution.py:278
  75.1 6.7 %collective-permute-start.6 = (f32[4,4,256]{2,1,0:T(4,128)S(1)}, f32[4,4,256]{2,1,0:T(4,128)S(1)}, u32[]{:S(2)}, u32[]{:S(2)}) collective-permute-start(f32[4,4,256]{2,1,0:T(4,128)S(1)} %slice.67), channel_id=1, source_target_pairs={{0,1},{1,2},{2,3},{3,0},{4,5},{5,6},{6,7},{7,4},{8,9},{9,10},{10,1... | collective-permute-start | bytes 49160 | tf_op jit(solution)/shard_map/ppermute | solution.py:317
  77.2 5.5 %collective-permute-start.7 = (f32[4,4,256]{2,1,0:T(4,128)S(1)}, f32[4,4,256]{2,1,0:T(4,128)S(1)}, u32[]{:S(2)}, u32[]{:S(2)}) collective-permute-start(f32[4,4,256]{2,1,0:T(4,128)S(1)} %slice.69), channel_id=1, source_target_pairs={{0,2},{1,3},{2,0},{3,1},{4,6},{5,7},{6,4},{7,5},{8,10},{9,11},{10,... | collective-permute-start | bytes 49160 | tf_op jit(solution)/shard_map/ppermute | solution.py:317
  80.8 3.7 %collective-permute-start.8 = (f32[4,4,256]{2,1,0:T(4,128)S(1)}, f32[4,4,256]{2,1,0:T(4,128)S(1)}, u32[]{:S(2)}, u32[]{:S(2)}) collective-permute-start(f32[4,4,256]{2,1,0:T(4,128)S(1)} %slice.71), channel_id=1, source_target_pairs={{0,3},{1,0},{2,1},{3,2},{4,7},{5,4},{6,5},{7,6},{8,11},{9,8},{10,9... | collective-permute-start | bytes 49160 | tf_op jit(solution)/shard_map/ppermute | solution.py:317

commit v3 on v2

v3 whole, which is shorter than its diff:
```python
import functools
import math

import jax
import jax.numpy as jnp
from jax import lax
from jax.experimental import pallas as pl
from jax.experimental.pallas import tpu as pltpu
from jax.sharding import PartitionSpec as P

BANDS = 8
HALF = BANDS // 2
UNITS = 16
FEATS = 4
OUTS = 12
SLAB = 16
LOG2E = math.log2(math.e)
F32 = jnp.float32
BF16 = jnp.bfloat16


def iota(shape, dim):
    return lax.broadcasted_iota(jnp.int32, shape, dim)


def split(value):
    high = value.astype(BF16)
    return high, (value - high.astype(F32)).astype(BF16)


def exact_dot(a, b):
    return jnp.dot(a, b, precision=lax.Precision.HIGHEST, preferred_element_type=F32)


def one_hot(shape, condition):
    return jnp.where(condition, jnp.ones(shape, F32), jnp.zeros(shape, F32))


def bias_columns(column):
    rows = column.shape[0]
    high = column.astype(BF16).astype(F32)
    rest = column - high
    middle = rest.astype(BF16).astype(F32)
    low = rest - middle
    lane = iota((rows, 16), 1)
    zero = jnp.zeros((rows, 16), F32)
    return jnp.where(
        lane == 0, high, jnp.where(lane == 1, middle, jnp.where(lane == 2, low, zero))
    ).astype(BF16)


def build_first(w_in, b_in):
    rows, cols = SLAB * UNITS, FEATS * SLAB
    pick = one_hot((rows, UNITS), iota((rows, UNITS), 0) % UNITS == iota((rows, UNITS), 1))
    spread = one_hot((FEATS, cols), iota((FEATS, cols), 1) // SLAB == iota((FEATS, cols), 0))
    full = exact_dot(exact_dot(pick, w_in), spread)
    full = jnp.where(iota((rows, cols), 0) // UNITS == iota((rows, cols), 1) % SLAB, full, 0.0)
    high, low = split(full)
    bias = bias_columns(jnp.sum(pick * b_in, axis=1, keepdims=True))
    return high, low, bias


def build_second(w_out, b_out):
    rows, cols = OUTS * 8, 8 * UNITS
    pick = one_hot((rows, OUTS), iota((rows, OUTS), 0) // 8 == iota((rows, OUTS), 1))
    spread = one_hot((UNITS, cols), iota((UNITS, cols), 1) % UNITS == iota((UNITS, cols), 0))
    full = exact_dot(exact_dot(pick, w_out), spread)
    full = jnp.where(iota((rows, cols), 0) % 8 == iota((rows, cols), 1) // UNITS, full, 0.0)
    out = iota((rows, 1), 0) // 8
    scale = jnp.where((out >= BANDS) & (out < BANDS + 3), -LOG2E, 1.0)
    high, low = split(full * scale)
    bias = bias_columns(jnp.sum(pick * b_out, axis=1, keepdims=True) * scale)
    return high, low, bias


def softplus(x):
    return jnp.maximum(jnp.log(1.0 + jnp.exp(jnp.minimum(x, 80.0))), x)


def front_kernel(total_x, total_z, batch, unroll, f_ref, win_ref, bin_ref, wout_ref, bout_ref, depth_ref, core_ref,
                 mid_ref, send_ref, keep_ref, dep_ref, first_ref, second_ref, tri_ref):
    cells_x = f_ref.shape[1]
    step = pl.program_id(0)
    core = core_ref[0]

    @pl.when(step == 0)
    def _():
        high, low, bias = build_first(win_ref[...].T, bin_ref[...])
        first_ref[:, 0:64] = high
        first_ref[:, 64:128] = high
        first_ref[:, 128:192] = low
        first_ref[:, 192:208] = bias
        high, low, bias = build_second(wout_ref[...], bout_ref[...])
        second_ref[:, 0:128] = high
        second_ref[:, 128:256] = high
        second_ref[:, 256:384] = low
        second_ref[:, 384:400] = bias
        tri_ref[...] = one_hot((256, 128), iota((256, 128), 0) % 128 < iota((256, 128), 1)).astype(BF16)

    ones = jnp.ones((16, 128 * batch), BF16)
    rates = [depth_ref[b] * (-LOG2E / total_x) for b in range(BANDS)]
    fade = -LOG2E / total_z

    y0 = pl.multiple_of(step * SLAB, SLAB)

    def layer_one(x0):
        rows = jnp.concatenate(
            [jnp.concatenate([f_ref[c, x0 + s] for s in range(batch)], axis=1) for c in range(FEATS)], axis=0
        )
        high, low = split(rows)
        return jnp.dot(first_ref[...], jnp.concatenate([high, low, high, ones], axis=0),
                       preferred_element_type=F32)

    def layer_two(hidden):
        high, low = split(jnp.maximum(hidden, 0.0))
        raws = []
        for j in range(2):
            part = slice(j * 128, j * 128 + 128)
            raws.append(jnp.dot(second_ref[...],
                                jnp.concatenate([high[part], low[part], high[part], ones], axis=0),
                                preferred_element_type=F32))
        return raws

    lane = iota((8, 128), 1)
    each = 128 // (2 * cells_x)

    def finish(x0, raws, sums, depth):
        sums = list(sums)
        for j in range(2):
            here = pl.ds(pl.multiple_of(y0 + 8 * j, 8), 8)
            for s in range(batch):
                x = x0 + s
                tile = raws[j][:, s * 128 : s * 128 + 128]
                for b in range(BANDS):
                    total = sums[j * BANDS + b]
                    mid_ref[b, x, here, :] = jnp.exp2(total * rates[b])
                    sums[j * BANDS + b] = total + softplus(tile[8 * b : 8 * b + 8])
                for k in range(BANDS, BANDS + 3):
                    mid_ref[k, x, here, :] = pl.reciprocal(
                        1.0 + jnp.exp2(tile[8 * k : 8 * k + 8]), approx=True)
                kappa = softplus(tile[8 * BANDS + 24 : 8 * BANDS + 32])
                mid_ref[BANDS + 3, x, here, :] = kappa
                column = jnp.sum(kappa, axis=1, keepdims=True)
                depth = jnp.where(lane == (step % each * 2 + j) * cells_x + x, column, depth)
        return tuple(sums), depth

    zero = jnp.zeros((8, 128), F32)
    sums, depth = (zero,) * (2 * BANDS), zero
    count = cells_x // batch
    hidden, raws = {}, {}
    for t in range(count + unroll):
        if t < count:
            hidden[t] = layer_one(t * batch)
        if unroll == 2 and 1 <= t <= count:
            raws[t - 1] = layer_two(hidden.pop(t - 1))
        if t >= unroll:
            if unroll == 1:
                raws[t - 1] = layer_two(hidden.pop(t - 1))
            sums, depth = finish((t - unroll) * batch, raws.pop(t - unroll), sums, depth)
    for j in range(2):
        for b in range(HALF):
            low, high = sums[j * BANDS + b], sums[j * BANDS + HALF + b]
            send_ref[b, 8 * j : 8 * j + 8, :] = jnp.where(core == 0, high, low)
            keep_ref[b, 8 * j : 8 * j + 8, :] = jnp.where(core == 0, low, high)
        here = pl.ds(pl.multiple_of(y0 + 8 * j, 8), 8)
        kappa = mid_ref[BANDS + 3, :, here, :].reshape(8 * cells_x, 128)
        both = jnp.concatenate(split(kappa), axis=1)
        occlusion = jnp.dot(both, tri_ref[...], preferred_element_type=F32)
        weight = jnp.exp2(occlusion * fade) * (1.0 - jnp.exp2(kappa * fade))
        mid_ref[BANDS + 3, :, here, :] = weight.reshape(cells_x, 8, 128)
    depth = depth * (1.0 / total_z)

    @pl.when(step % each == 0)
    def _():
        dep_ref[0] = depth

    @pl.when(step % each != 0)
    def _():
        dep_ref[0] = dep_ref[0] + depth


def back_kernel(total_x, unroll, mid_ref, mine_ref, theirs_ref, dep_ref, depth_ref, core_ref, mix_ref,
                light_ref, *img_refs):
    cells_x = light_ref.shape[1]
    ndev = len(img_refs)
    each = pl.num_programs(0) // ndev
    step = pl.program_id(0)
    apart = (step // each - core_ref[5] + ndev) % ndev
    lane = iota((8, 128), 1)
    colours = (jnp.zeros((8, 128), F32),) * 3
    for j in range(2):
        here = slice(8 * j, 8 * j + 8)
        deep = pl.ds(pl.multiple_of(pl.program_id(0) * SLAB + 8 * j, 8), 8)
        gains = []
        for b in range(BANDS):
            mine, theirs = mine_ref[b % HALF, here], theirs_ref[b % HALF, here]
            before = jnp.where(core_ref[0] == b // HALF, mine, theirs)
            fade = jnp.exp2(before * (depth_ref[b] * (-LOG2E / total_x)))
            gains.append([fade * mix_ref[k, b] for k in range(3)])
        first = (step % each * 2 + j) * cells_x

        def one(x, colours):
            bands = [mid_ref[b, x, deep, :] for b in range(BANDS)]
            weight = mid_ref[BANDS + 3, x, deep, :]
            place = lane == first + x
            result = []
            for k in range(3):
                total = bands[0] * gains[0][k]
                for b in range(1, BANDS):
                    total = total + bands[b] * gains[b][k]
                light = total * mid_ref[BANDS + k, x, deep, :]
                light_ref[k, x, here, :] = light
                column = jnp.sum(light * weight, axis=1, keepdims=True)
                result.append(jnp.where(place, column, colours[k]))
            return tuple(result)

        colours = lax.fori_loop(0, cells_x, one, colours, unroll=unroll)
    for other in range(ndev):
        @pl.when((apart == other) & (step % each == 0))
        def _():
            for k in range(3):
                img_refs[other][k] = colours[k]
            img_refs[other][3] = dep_ref[0]

        @pl.when((apart == other) & (step % each != 0))
        def _():
            for k in range(3):
                img_refs[other][k] = img_refs[other][k] + colours[k]


def front(features, w_in, b_in, w_out, b_out, band_depth, place, total_x, total_z, first, rows_y):
    _, cells_x, _, cells_z = features.shape
    skip = first // SLAB
    each = 128 // (2 * cells_x)

    whole = pl.BlockSpec(memory_space=pltpu.VMEM)

    def small(*shape):
        return pl.BlockSpec(shape, lambda i: (0,) * len(shape))

    return pl.pallas_call(
        functools.partial(front_kernel, total_x, total_z, 2, 2),
        grid=(rows_y // SLAB,),
        in_specs=[
            pl.BlockSpec((FEATS, cells_x, SLAB, cells_z), lambda i: (0, 0, i + skip, 0)),
            small(FEATS, UNITS), small(1, UNITS), small(OUTS, UNITS), small(1, OUTS),
            pl.BlockSpec(memory_space=pltpu.SMEM),
            pl.BlockSpec(memory_space=pltpu.SMEM),
        ],
        out_specs=[
            whole,
            pl.BlockSpec((HALF, SLAB, cells_z), lambda i: (0, i, 0)),
            pl.BlockSpec((HALF, SLAB, cells_z), lambda i: (0, i, 0)),
            pl.BlockSpec((1, 8, 128), lambda i: (i // each, 0, 0)),
        ],
        out_shape=[
            pltpu.MemorySpace.VMEM((OUTS, cells_x, rows_y, cells_z), F32),
            jax.ShapeDtypeStruct((HALF, rows_y, cells_z), F32),
            jax.ShapeDtypeStruct((HALF, rows_y, cells_z), F32),
            jax.ShapeDtypeStruct((rows_y // SLAB // each, 8, 128), F32),
        ],
        scratch_shapes=[
            pltpu.VMEM((SLAB * UNITS, 208), BF16),
            pltpu.VMEM((OUTS * 8, 400), BF16),
            pltpu.VMEM((256, 128), BF16),
        ],
        compiler_params=pltpu.CompilerParams(vmem_limit_bytes=16 << 20),
        name="front",
    )(*(pltpu.with_memory_space_constraint(value, pltpu.HBM)
        for value in (features, w_in.T, b_in[None], w_out, b_out[None])), band_depth, place)


def back(mid, incoming, dep, band_depth, place, band_mix, total_x, ndev):
    _, cells_x, rows_y, cells_z = mid.shape
    slabs = rows_y // SLAB
    each = slabs // ndev
    scalar = pl.BlockSpec(memory_space=pltpu.SMEM)
    whole = pl.BlockSpec(memory_space=pltpu.VMEM)
    return pl.pallas_call(
        functools.partial(back_kernel, total_x, cells_x),
        grid=(slabs,),
        in_specs=[
            whole,
            pl.BlockSpec((HALF, SLAB, cells_z), lambda i: (0, i, 0)),
            pl.BlockSpec((HALF, SLAB, cells_z), lambda i: (0, i, 0)),
            pl.BlockSpec((1, 8, 128), lambda i: (i // each, 0, 0)),
            scalar, scalar, scalar,
        ],
        out_specs=[pl.BlockSpec((3, cells_x, SLAB, cells_z), lambda i: (0, 0, i, 0))] + [whole] * ndev,
        out_shape=[jax.ShapeDtypeStruct((3, cells_x, rows_y, cells_z), F32)]
        + [jax.ShapeDtypeStruct((4, 8, 128), F32)] * ndev,
        compiler_params=pltpu.CompilerParams(vmem_limit_bytes=16 << 20),
        name="back",
    )(pltpu.with_memory_space_constraint(mid, pltpu.VMEM), *incoming, dep, band_depth, place, band_mix)


def swap(value, axis, partner):
    return lax.ppermute(value, axis, [(i, partner(i)) for i in range(lax.axis_size(axis))])


def across(i, bit):
    return i ^ 1 if bit == 0 else 3 - i


def small_kernel(body, arrays, place, outputs):
    whole = pl.BlockSpec(memory_space=pltpu.VMEM)
    shape = arrays[0].shape

    def kernel(place_ref, *refs):
        where = [place_ref[i] for i in range(6)]
        for band in range(shape[0]):
            values = [ref[band] for ref in refs[: len(arrays)]]
            for ref, value in zip(refs[len(arrays) :], body(where, *values), strict=True):
                ref[band] = value

    return pl.pallas_call(
        kernel,
        in_specs=[pl.BlockSpec(memory_space=pltpu.SMEM)] + [whole] * len(arrays),
        out_specs=[whole] * outputs,
        out_shape=[jax.ShapeDtypeStruct(shape, F32)] * outputs,
        compiler_params=pltpu.CompilerParams(vmem_limit_bytes=4 << 20),
        name="combine",
    )(place, *arrays)


def scan_x(send, keep, place):
    got = swap(send, "gx", lambda i: i ^ 1)
    (total,) = small_kernel(lambda where, a, b: [a + b], [keep, got], place, 1)
    before = None
    for stage in range(4):
        axis, bit = divmod(stage, 2)

        def partner(i):
            if axis == 0:
                return i // 8 * 8 + across(i // 2 % 4, bit) * 2 + i % 2
            return across(i // 8, bit) * 8 + i % 8

        other = swap(total, "gx", partner)

        def merge(where, total, other, before=0.0):
            return [total + other, before + jnp.where(where[1 + stage] == 1, other, 0.0)]

        def last(where, other, before, keep, got):
            before = before + jnp.where(where[1 + stage] == 1, other, 0.0)
            return [before + jnp.where(where[0] == 0, 0.0, got), before + jnp.where(where[0] == 0, keep, 0.0)]

        if stage < 3:
            total, before = small_kernel(merge, [total, other] + ([before] if stage else []), place, 2)
        else:
            mine, theirs = small_kernel(last, [other, before, keep, got], place, 2)
    return mine, swap(theirs, "gx", lambda i: i ^ 1)


def compose_kernel(place_ref, *refs):
    pieces, out_ref = refs[:-1], refs[-1]
    ndev = len(pieces)
    origin = [(place_ref[5] - apart + ndev) % ndev for apart in range(ndev)]
    depths = [piece[3] for piece in pieces]
    totals = [jnp.zeros_like(depths[0])] * 3
    for i in range(ndev):
        ahead = jnp.zeros_like(depths[0])
        for j in range(ndev):
            if j != i:
                ahead = ahead + jnp.where(origin[j] < origin[i], depths[j], 0.0)
        through = jnp.exp(-ahead)
        totals = [total + through * pieces[i][k] for k, total in enumerate(totals)]
    for k in range(3):
        out_ref[k] = totals[k]
    out_ref[3] = 1.0 - jnp.exp(-sum(depths[1:], depths[0]))


def composite(pieces, place, cells_x):
    ndev = len(pieces)
    held = [
        lax.ppermute(piece, "gz", [(i, (i + apart) % ndev) for i in range(ndev)]) if apart else piece
        for apart, piece in enumerate(pieces)
    ]
    whole = pl.BlockSpec(memory_space=pltpu.VMEM)
    image = pl.pallas_call(
        compose_kernel,
        in_specs=[pl.BlockSpec(memory_space=pltpu.SMEM)] + [whole] * ndev,
        out_specs=whole,
        out_shape=jax.ShapeDtypeStruct(pieces[0].shape, F32),
        compiler_params=pltpu.CompilerParams(vmem_limit_bytes=4 << 20),
        name="compose",
    )(place, *held)
    image = image.reshape(4, 8, 128 // cells_x, cells_x)
    return image.transpose(0, 3, 2, 1).reshape(4, cells_x, -1)


def body(features, w_in, b_in, w_out, b_out, band_depth, band_mix):
    cells_x = features.shape[1]
    total_x = cells_x * lax.axis_size("gx")
    total_z = features.shape[3] * lax.axis_size("gz")
    rows_y = features.shape[2]
    me = lax.axis_index("gx")
    place = jnp.stack([me % 2, me // 2 % 2, me // 4 % 2, me // 8 % 2, me // 16 % 2,
                       lax.axis_index("gz")]).astype(jnp.int32)
    mid, send, keep, dep = front(
        features, w_in, b_in, w_out, b_out, band_depth, place, total_x, total_z, 0, rows_y)
    incoming = scan_x(send, keep, place)
    light, *pieces = back(mid, incoming, dep, band_depth, place, band_mix, total_x, lax.axis_size("gz"))
    return light, composite(pieces, place, cells_x)


def solution(mesh):
    in_specs = (P(None, "gx", None, "gz"), P(), P(), P(), P(), P(), P())
    out_specs = (P(None, "gx", None, "gz"), P(None, "gx", "gz"))
    return jax.shard_map(body, mesh=mesh, in_specs=in_specs, out_specs=out_specs, check_vma=False)
```

time: 86 us -> 79.4 us (0.923)
  Pallas kernels: 38.5 us -> 32.8 us
    pallas_call x2 -> x8, Pallas kernels: 38.5 us -> 32.8 us  [the longest x1 21.8 us: front(): pl.pallas_call(functools.partial(front_kernel, total_x, total_z, 2, 2), g...]
where the time goes in v3:
time: 79.4 us; the launch traced here: 79.3 us
  Pallas kernels  32.8 us (41%)
  waiting for transfers between devices  27.8 us (35%)
  starting transfers between devices  16.3 us (21%)
  local copies, waits for them, and re-layouts  1.56 us (2%)
  between operations  0.83 us (1%)
    ppermute x6, waiting for transfers between devices, swap(): lax.ppermute(value, axis, [(i, partner(i)) for i in range(lax.axis_size(a...  25.1 us
    pallas_call x1, Pallas kernels, front(): pl.pallas_call(functools.partial(front_kernel, total_x, total_z, 2, 2), g...  21.8 us
    ppermute x6, starting transfers between devices, swap(): lax.ppermute(value, axis, [(i, partner(i)) for i in range(lax.axis_size(a...  9.68 us
    pallas_call x1, Pallas kernels, back(): pl.pallas_call(functools.partial(back_kernel, total_x, cells_x), grid=(sl...  7.49 us
    ppermute x3, starting transfers between devices, composite(): lax.ppermute(piece, 'gz', [(i, (i + apart) % ndev) for i in range(ndev)])  6.59 us
    pallas_call x5, Pallas kernels, small_kernel(): pl.pallas_call(kernel, in_specs=[pl.BlockSpec(memory_space=pltpu.SMEM)] +...  2.94 us
    ppermute x3, waiting for transfers between devices, composite(): lax.ppermute(piece, 'gz', [(i, (i + apart) % ndev) for i in range(ndev)])  2.73 us
  transfers between devices with their start and end apart: 9, of which 8 were waited for; matrix products, arithmetic and copies ran while one was open for 0% of the time, Pallas kernels for 0%

profile of v3, /device:TPU:0, one launch (start us, length us, event | category | flops | bytes accessed | tf_op | source)
XLA Modules:
  0.0 79.3 jit_solution(17243301757523408210)
XLA Ops:
  0.8 0.7 copy-done.1
  1.5 21.8 %front.1 = (f32[12,32,128,128]{3,2,1,0:T(8,128)S(1)}, f32[4,128,128]{2,1,0:T(8,128)S(1)}, f32[4,128,128]{2,1,0:T(8,128)S(1)}, f32[4,8,128]{2,1,0:T(8,128)S(1)}) custom-call(f32[4,32,128,128]{3,2,1,0:T(8,128)} %f_ref.1, f32[4,16]{1,0:T(4,128)} %bitcast.15, f32[1,16]{1,0:T(1,128)} %bitcast.16, f32[12,16]{1,0:T(8,128)} %wout_ref.1, f32[1,12]{1,0:T(1,128)} %bitcast.17, ...), custom_call_target="tpu_custom_call" | custom-call | tf_op jit(solution)/shard_map/front/pallas_call | solution.py:241
  23.4 1.5 %collective-permute-done.refs_1_.refs_3_ = f32[4,128,128]{2,1,0:T(8,128)S(1)} collective-permute-done((f32[4,128,128]{2,1,0:T(8,128)S(1)}, f32[4,128,128]{2,1,0:T(8,128)S(1)}, u32[]{:S(2)}, u32[]{:S(2)}) %collective-permute-start) | collective-permute-done | bytes 262176 | tf_op jit(solution)/shard_map/ppermute | solution.py:298
  25.5 1.7 %collective-permute-start.1 = (f32[4,128,128]{2,1,0:T(8,128)S(1)}, f32[4,128,128]{2,1,0:T(8,128)S(1)}, u32[]{:S(2)}, u32[]{:S(2)}) collective-permute-start(f32[4,128,128]{2,1,0:T(8,128)S(1)} %combine.5.refs_0_), channel_id=1, source_target_pairs={{0,8},{4,12},{8,0},{12,4},{16,24},{20,28},{24,16},{28,20},{32,40},... | collective-permute-start | bytes 786440 | tf_op jit(solution)/shard_map/ppermute | solution.py:298
  27.1 6.8 %collective-permute-done.1.refs_1_ = f32[4,128,128]{2,1,0:T(8,128)S(1)} collective-permute-done((f32[4,128,128]{2,1,0:T(8,128)S(1)}, f32[4,128,128]{2,1,0:T(8,128)S(1)}, u32[]{:S(2)}, u32[]{:S(2)}) %collective-permute-start.1) | collective-permute-done | bytes 262176 | tf_op jit(solution)/shard_map/ppermute | solution.py:298
  33.9 0.6 combine.6
  34.5 2.9 %collective-permute-start.2 = (f32[4,128,128]{2,1,0:T(8,128)S(1)}, f32[4,128,128]{2,1,0:T(8,128)S(1)}, u32[]{:S(2)}, u32[]{:S(2)}) collective-permute-start(f32[4,128,128]{2,1,0:T(8,128)S(1)} %get-tuple-element.22.refs_0_), channel_id=1, source_target_pairs={{0,24},{4,28},{8,16},{12,20},{16,8},{20,12},{24,0},{28,4},{32,56},... | collective-permute-start | bytes 786440 | tf_op jit(solution)/shard_map/ppermute | solution.py:298
  37.4 5.9 %collective-permute-done.2.refs_1_ = f32[4,128,128]{2,1,0:T(8,128)S(1)} collective-permute-done((f32[4,128,128]{2,1,0:T(8,128)S(1)}, f32[4,128,128]{2,1,0:T(8,128)S(1)}, u32[]{:S(2)}, u32[]{:S(2)}) %collective-permute-start.2) | collective-permute-done | bytes 262176 | tf_op jit(solution)/shard_map/ppermute | solution.py:298
  43.3 0.6 combine.7
  43.9 1.7 %collective-permute-start.3 = (f32[4,128,128]{2,1,0:T(8,128)S(1)}, f32[4,128,128]{2,1,0:T(8,128)S(1)}, u32[]{:S(2)}, u32[]{:S(2)}) collective-permute-start(f32[4,128,128]{2,1,0:T(8,128)S(1)} %get-tuple-element.24.refs_0_), channel_id=1, source_target_pairs={{0,32},{4,36},{8,40},{12,44},{16,48},{20,52},{24,56},{28,60},{32,0... | collective-permute-start | bytes 786440 | tf_op jit(solution)/shard_map/ppermute | solution.py:298
  45.6 4.9 %collective-permute-done.3.refs_1_ = f32[4,128,128]{2,1,0:T(8,128)S(1)} collective-permute-done((f32[4,128,128]{2,1,0:T(8,128)S(1)}, f32[4,128,128]{2,1,0:T(8,128)S(1)}, u32[]{:S(2)}, u32[]{:S(2)}) %collective-permute-start.3) | collective-permute-done | bytes 262176 | tf_op jit(solution)/shard_map/ppermute | solution.py:298
  50.6 0.6 combine.8
  51.2 3.2 %collective-permute-start.4 = (f32[4,128,128]{2,1,0:T(8,128)S(1)}, f32[4,128,128]{2,1,0:T(8,128)S(1)}, u32[]{:S(2)}, u32[]{:S(2)}) collective-permute-start(f32[4,128,128]{2,1,0:T(8,128)S(1)} %get-tuple-element.26), channel_id=1, source_target_pairs={{0,96},{4,100},{8,104},{12,108},{16,112},{20,116},{24,120},{28,124... | collective-permute-start | bytes 786440 | tf_op jit(solution)/shard_map/ppermute | solution.py:298
  54.3 4.5 %collective-permute-done.4.refs_0_ = f32[4,128,128]{2,1,0:T(8,128)S(1)} collective-permute-done((f32[4,128,128]{2,1,0:T(8,128)S(1)}, f32[4,128,128]{2,1,0:T(8,128)S(1)}, u32[]{:S(2)}, u32[]{:S(2)}) %collective-permute-start.4) | collective-permute-done | bytes 262176 | tf_op jit(solution)/shard_map/ppermute | solution.py:298
  58.8 0.6 combine.9
  59.5 1.5 %collective-permute-done.5.theirs_ref = f32[4,128,128]{2,1,0:T(8,128)S(1)} collective-permute-done((f32[4,128,128]{2,1,0:T(8,128)S(1)}, f32[4,128,128]{2,1,0:T(8,128)S(1)}, u32[]{:S(2)}, u32[]{:S(2)}) %collective-permute-start.5) | collective-permute-done | bytes 262176 | tf_op jit(solution)/shard_map/ppermute | solution.py:298
  61.1 7.5 %back.1 = (f32[3,32,128,128]{3,2,1,0:T(8,128)}, f32[4,8,128]{2,1,0:T(8,128)S(1)}, f32[4,8,128]{2,1,0:T(8,128)S(1)}, f32[4,8,128]{2,1,0:T(8,128)S(1)}, f32[4,8,128]{2,1,0:T(8,128)S(1)}) custom-call(f32[12,32,128,128]{3,2,1,0:T(8,128)S(1)} %get-tuple-element.19.mid_ref, f32[4,128,128]{2,1,0:T(8,128)S(1)} %get-tuple-element.28.mine_ref, ...), custom_call_target="tpu_custom_call" | custom-call | tf_op jit(solution)/shard_map/back/pallas_call | solution.py:279
  68.6 2.0 %collective-permute-start.6 = (f32[4,8,128]{2,1,0:T(8,128)S(1)}, f32[4,8,128]{2,1,0:T(8,128)S(1)}, u32[]{:S(2)}, u32[]{:S(2)}) collective-permute-start(f32[4,8,128]{2,1,0:T(8,128)S(1)} %get-tuple-element.33), channel_id=1, source_target_pairs={{0,1},{1,2},{2,3},{3,0},{4,5},{5,6},{6,7},{7,4},{8,9},{9,10},{10,1... | collective-permute-start | bytes 49160 | tf_op jit(solution)/shard_map/ppermute | solution.py:375
  70.6 3.6 %collective-permute-start.7 = (f32[4,8,128]{2,1,0:T(8,128)S(1)}, f32[4,8,128]{2,1,0:T(8,128)S(1)}, u32[]{:S(2)}, u32[]{:S(2)}) collective-permute-start(f32[4,8,128]{2,1,0:T(8,128)S(1)} %get-tuple-element.34), channel_id=1, source_target_pairs={{0,2},{1,3},{2,0},{3,1},{4,6},{5,7},{6,4},{7,5},{8,10},{9,11},{10,... | collective-permute-start | bytes 49160 | tf_op jit(solution)/shard_map/ppermute | solution.py:375
  74.1 1.0 %collective-permute-start.8 = (f32[4,8,128]{2,1,0:T(8,128)S(1)}, f32[4,8,128]{2,1,0:T(8,128)S(1)}, u32[]{:S(2)}, u32[]{:S(2)}) collective-permute-start(f32[4,8,128]{2,1,0:T(8,128)S(1)} %get-tuple-element.35), channel_id=1, source_target_pairs={{0,3},{1,0},{2,1},{3,2},{4,7},{5,4},{6,5},{7,6},{8,11},{9,8},{10,9... | collective-permute-start | bytes 49160 | tf_op jit(solution)/shard_map/ppermute | solution.py:375
  75.2 0.9 %collective-permute-done.7.refs_2_ = f32[4,8,128]{2,1,0:T(8,128)S(1)} collective-permute-done((f32[4,8,128]{2,1,0:T(8,128)S(1)}, f32[4,8,128]{2,1,0:T(8,128)S(1)}, u32[]{:S(2)}, u32[]{:S(2)}) %collective-permute-start.7) | collective-permute-done | bytes 16416 | tf_op jit(solution)/shard_map/ppermute | solution.py:375
  76.0 1.9 %collective-permute-done.8.refs_3_ = f32[4,8,128]{2,1,0:T(8,128)S(1)} collective-permute-done((f32[4,8,128]{2,1,0:T(8,128)S(1)}, f32[4,8,128]{2,1,0:T(8,128)S(1)}, u32[]{:S(2)}, u32[]{:S(2)}) %collective-permute-start.8) | collective-permute-done | bytes 16416 | tf_op jit(solution)/shard_map/ppermute | solution.py:375
  77.9 0.6 compose.1
  78.6 0.7 copy.11
  (10 shorter events, 0.9 us)
Async XLA Ops:
  0.6 60.4 %copy-start = (f32[3,8]{1,0:T(4,128)S(1)}, f32[3,8]{1,0:T(4,128)}, u32[]{:S(2)}) copy-start(f32[3,8]{1,0:T(4,128)} %mix_ref.1) | copy-start | bytes 292
  0.8 0.7 copy-start.1
  23.3 1.6 %collective-permute-start = (f32[4,128,128]{2,1,0:T(8,128)S(1)}, f32[4,128,128]{2,1,0:T(8,128)S(1)}, u32[]{:S(2)}, u32[]{:S(2)}) collective-permute-start(f32[4,128,128]{2,1,0:T(8,128)S(1)} %get-tuple-element.21), channel_id=1, source_target_pairs={{0,4},{4,0},{8,12},{12,8},{16,20},{20,16},{24,28},{28,24},{32,36},... | collective-permute-start | bytes 786440 | tf_op jit(solution)/shard_map/ppermute | solution.py:298
  25.5 8.4 %collective-permute-start.1 = (f32[4,128,128]{2,1,0:T(8,128)S(1)}, f32[4,128,128]{2,1,0:T(8,128)S(1)}, u32[]{:S(2)}, u32[]{:S(2)}) collective-permute-start(f32[4,128,128]{2,1,0:T(8,128)S(1)} %combine.5.refs_0_), channel_id=1, source_target_pairs={{0,8},{4,12},{8,0},{12,4},{16,24},{20,28},{24,16},{28,20},{32,40},... | collective-permute-start | bytes 786440 | tf_op jit(solution)/shard_map/ppermute | solution.py:298
  34.5 8.8 %collective-permute-start.2 = (f32[4,128,128]{2,1,0:T(8,128)S(1)}, f32[4,128,128]{2,1,0:T(8,128)S(1)}, u32[]{:S(2)}, u32[]{:S(2)}) collective-permute-start(f32[4,128,128]{2,1,0:T(8,128)S(1)} %get-tuple-element.22.refs_0_), channel_id=1, source_target_pairs={{0,24},{4,28},{8,16},{12,20},{16,8},{20,12},{24,0},{28,4},{32,56},... | collective-permute-start | bytes 786440 | tf_op jit(solution)/shard_map/ppermute | solution.py:298
  43.9 6.7 %collective-permute-start.3 = (f32[4,128,128]{2,1,0:T(8,128)S(1)}, f32[4,128,128]{2,1,0:T(8,128)S(1)}, u32[]{:S(2)}, u32[]{:S(2)}) collective-permute-start(f32[4,128,128]{2,1,0:T(8,128)S(1)} %get-tuple-element.24.refs_0_), channel_id=1, source_target_pairs={{0,32},{4,36},{8,40},{12,44},{16,48},{20,52},{24,56},{28,60},{32,0... | collective-permute-start | bytes 786440 | tf_op jit(solution)/shard_map/ppermute | solution.py:298
  51.2 7.7 %collective-permute-start.4 = (f32[4,128,128]{2,1,0:T(8,128)S(1)}, f32[4,128,128]{2,1,0:T(8,128)S(1)}, u32[]{:S(2)}, u32[]{:S(2)}) collective-permute-start(f32[4,128,128]{2,1,0:T(8,128)S(1)} %get-tuple-element.26), channel_id=1, source_target_pairs={{0,96},{4,100},{8,104},{12,108},{16,112},{20,116},{24,120},{28,124... | collective-permute-start | bytes 786440 | tf_op jit(solution)/shard_map/ppermute | solution.py:298
  59.4 1.6 %collective-permute-start.5 = (f32[4,128,128]{2,1,0:T(8,128)S(1)}, f32[4,128,128]{2,1,0:T(8,128)S(1)}, u32[]{:S(2)}, u32[]{:S(2)}) collective-permute-start(f32[4,128,128]{2,1,0:T(8,128)S(1)} %get-tuple-element.29), channel_id=1, source_target_pairs={{0,4},{4,0},{8,12},{12,8},{16,20},{20,16},{24,28},{28,24},{32,36},... | collective-permute-start | bytes 786440 | tf_op jit(solution)/shard_map/ppermute | solution.py:298
  68.6 6.6 %collective-permute-start.6 = (f32[4,8,128]{2,1,0:T(8,128)S(1)}, f32[4,8,128]{2,1,0:T(8,128)S(1)}, u32[]{:S(2)}, u32[]{:S(2)}) collective-permute-start(f32[4,8,128]{2,1,0:T(8,128)S(1)} %get-tuple-element.33), channel_id=1, source_target_pairs={{0,1},{1,2},{2,3},{3,0},{4,5},{5,6},{6,7},{7,4},{8,9},{9,10},{10,1... | collective-permute-start | bytes 49160 | tf_op jit(solution)/shard_map/ppermute | solution.py:375
  70.6 5.5 %collective-permute-start.7 = (f32[4,8,128]{2,1,0:T(8,128)S(1)}, f32[4,8,128]{2,1,0:T(8,128)S(1)}, u32[]{:S(2)}, u32[]{:S(2)}) collective-permute-start(f32[4,8,128]{2,1,0:T(8,128)S(1)} %get-tuple-element.34), channel_id=1, source_target_pairs={{0,2},{1,3},{2,0},{3,1},{4,6},{5,7},{6,4},{7,5},{8,10},{9,11},{10,... | collective-permute-start | bytes 49160 | tf_op jit(solution)/shard_map/ppermute | solution.py:375
  74.1 3.7 %collective-permute-start.8 = (f32[4,8,128]{2,1,0:T(8,128)S(1)}, f32[4,8,128]{2,1,0:T(8,128)S(1)}, u32[]{:S(2)}, u32[]{:S(2)}) collective-permute-start(f32[4,8,128]{2,1,0:T(8,128)S(1)} %get-tuple-element.35), channel_id=1, source_target_pairs={{0,3},{1,0},{2,1},{3,2},{4,7},{5,4},{6,5},{7,6},{8,11},{9,8},{10,9... | collective-permute-start | bytes 49160 | tf_op jit(solution)/shard_map/ppermute | solution.py:375

commit v4 on v3

--- a/solution.py
+++ b/solution.py
@@ -10,6 +10,8 @@
 
 BANDS = 8
 HALF = BANDS // 2
+PIECES = 2
+EACH = HALF // PIECES
 UNITS = 16
 FEATS = 4
 OUTS = 12
@@ -78,8 +80,10 @@
 
 
 def front_kernel(total_x, total_z, batch, unroll, f_ref, win_ref, bin_ref, wout_ref, bout_ref, depth_ref, core_ref,
-                 mid_ref, send_ref, keep_ref, dep_ref, first_ref, second_ref, tri_ref):
+                 mid_ref, *rest):
     cells_x = f_ref.shape[1]
+    send_refs, keep_refs = rest[:PIECES], rest[PIECES : 2 * PIECES]
+    dep_ref, first_ref, second_ref, tri_ref = rest[2 * PIECES :]
     step = pl.program_id(0)
     core = core_ref[0]
 
@@ -160,8 +164,8 @@
     for j in range(2):
         for b in range(HALF):
             low, high = sums[j * BANDS + b], sums[j * BANDS + HALF + b]
-            send_ref[b, 8 * j : 8 * j + 8, :] = jnp.where(core == 0, high, low)
-            keep_ref[b, 8 * j : 8 * j + 8, :] = jnp.where(core == 0, low, high)
+            send_refs[b // EACH][b % EACH, 8 * j : 8 * j + 8, :] = jnp.where(core == 0, high, low)
+            keep_refs[b // EACH][b % EACH, 8 * j : 8 * j + 8, :] = jnp.where(core == 0, low, high)
         here = pl.ds(pl.multiple_of(y0 + 8 * j, 8), 8)
         kappa = mid_ref[BANDS + 3, :, here, :].reshape(8 * cells_x, 128)
         both = jnp.concatenate(split(kappa), axis=1)
@@ -179,8 +183,9 @@
         dep_ref[0] = dep_ref[0] + depth
 
 
-def back_kernel(total_x, unroll, mid_ref, mine_ref, theirs_ref, dep_ref, depth_ref, core_ref, mix_ref,
-                light_ref, *img_refs):
+def back_kernel(total_x, unroll, mid_ref, *rest):
+    mine_refs, theirs_refs = rest[:PIECES], rest[PIECES : 2 * PIECES]
+    dep_ref, depth_ref, core_ref, mix_ref, light_ref, *img_refs = rest[2 * PIECES :]
     cells_x = light_ref.shape[1]
     ndev = len(img_refs)
     each = pl.num_programs(0) // ndev
@@ -193,7 +198,8 @@
         deep = pl.ds(pl.multiple_of(pl.program_id(0) * SLAB + 8 * j, 8), 8)
         gains = []
         for b in range(BANDS):
-            mine, theirs = mine_ref[b % HALF, here], theirs_ref[b % HALF, here]
+            piece, band = divmod(b % HALF, EACH)
+            mine, theirs = mine_refs[piece][band, here], theirs_refs[piece][band, here]
             before = jnp.where(core_ref[0] == b // HALF, mine, theirs)
             fade = jnp.exp2(before * (depth_ref[b] * (-LOG2E / total_x)))
             gains.append([fade * mix_ref[k, b] for k in range(3)])
@@ -249,14 +255,12 @@
         ],
         out_specs=[
             whole,
-            pl.BlockSpec((HALF, SLAB, cells_z), lambda i: (0, i, 0)),
-            pl.BlockSpec((HALF, SLAB, cells_z), lambda i: (0, i, 0)),
+            *[pl.BlockSpec((EACH, SLAB, cells_z), lambda i: (0, i, 0))] * (2 * PIECES),
             pl.BlockSpec((1, 8, 128), lambda i: (i // each, 0, 0)),
         ],
         out_shape=[
             pltpu.MemorySpace.VMEM((OUTS, cells_x, rows_y, cells_z), F32),
-            jax.ShapeDtypeStruct((HALF, rows_y, cells_z), F32),
-            jax.ShapeDtypeStruct((HALF, rows_y, cells_z), F32),
+            *[jax.ShapeDtypeStruct((EACH, rows_y, cells_z), F32)] * (2 * PIECES),
             jax.ShapeDtypeStruct((rows_y // SLAB // each, 8, 128), F32),
         ],
         scratch_shapes=[
@@ -281,8 +285,7 @@
         grid=(slabs,),
         in_specs=[
             whole,
-            pl.BlockSpec((HALF, SLAB, cells_z), lambda i: (0, i, 0)),
-            pl.BlockSpec((HALF, SLAB, cells_z), lambda i: (0, i, 0)),
+            *[pl.BlockSpec((EACH, SLAB, cells_z), lambda i: (0, i, 0))] * (2 * PIECES),
             pl.BlockSpec((1, 8, 128), lambda i: (i // each, 0, 0)),
             scalar, scalar, scalar,
         ],
@@ -396,9 +399,10 @@
     me = lax.axis_index("gx")
     place = jnp.stack([me % 2, me // 2 % 2, me // 4 % 2, me // 8 % 2, me // 16 % 2,
                        lax.axis_index("gz")]).astype(jnp.int32)
-    mid, send, keep, dep = front(
+    mid, *sums, dep = front(
         features, w_in, b_in, w_out, b_out, band_depth, place, total_x, total_z, 0, rows_y)
-    incoming = scan_x(send, keep, place)
+    scanned = [scan_x(sums[i], sums[PIECES + i], place) for i in range(PIECES)]
+    incoming = [mine for mine, _ in scanned] + [theirs for _, theirs in scanned]
     light, *pieces = back(mid, incoming, dep, band_depth, place, band_mix, total_x, lax.axis_size("gz"))
     return light, composite(pieces, place, cells_x)
 

time: 79.4 us -> 77.3 us (0.974)
  waiting for transfers between devices: 27.8 us -> 16.9 us
  starting transfers between devices: 16.3 us -> 21.7 us
  Pallas kernels: 32.8 us -> 35.6 us
    ppermute x6 -> x12, waiting for transfers between devices: 25.1 us -> 14.2 us  [swap(): lax.ppermute(value, axis, [(i, partner(i)) for i in range(lax.axis_size(a...]
    ppermute x6 -> x12, starting transfers between devices: 9.68 us -> 15.2 us  [swap(): lax.ppermute(value, axis, [(i, partner(i)) for i in range(lax.axis_size(a...]
    pallas_call x5 -> x10, Pallas kernels: 2.94 us -> 5.66 us  [small_kernel(): pl.pallas_call(kernel, in_specs=[pl.BlockSpec(memory_space=pltpu.SMEM)] +...]
  transfers between devices with their start and end apart: 9 -> 15, of which waited for: 8 -> 10; matrix products, arithmetic and copies ran while one was open for 0% -> 0% of each run, Pallas kernels for 0% -> 7%
where the time goes in v4:
time: 77.3 us; the launch traced here: 76.6 us
  Pallas kernels  35.6 us (46%)
  starting transfers between devices  21.7 us (28%)
  waiting for transfers between devices  16.9 us (22%)
  local copies, waits for them, and re-layouts  1.56 us (2%)
  between operations  0.89 us (1%)
    pallas_call x1, Pallas kernels, front(): pl.pallas_call(functools.partial(front_kernel, total_x, total_z, 2, 2), g...  21.8 us
    ppermute x12, starting transfers between devices, swap(): lax.ppermute(value, axis, [(i, partner(i)) for i in range(lax.axis_size(a...  15.2 us
    ppermute x12, waiting for transfers between devices, swap(): lax.ppermute(value, axis, [(i, partner(i)) for i in range(lax.axis_size(a...  14.2 us
    pallas_call x1, Pallas kernels, back(): pl.pallas_call(functools.partial(back_kernel, total_x, cells_x), grid=(sl...  7.53 us
    ppermute x3, starting transfers between devices, composite(): lax.ppermute(piece, 'gz', [(i, (i + apart) % ndev) for i in range(ndev)])  6.53 us
    pallas_call x10, Pallas kernels, small_kernel(): pl.pallas_call(kernel, in_specs=[pl.BlockSpec(memory_space=pltpu.SMEM)] +...  5.66 us
    ppermute x3, waiting for transfers between devices, composite(): lax.ppermute(piece, 'gz', [(i, (i + apart) % ndev) for i in range(ndev)])  2.7 us
  transfers between devices with their start and end apart: 15, of which 10 were waited for; matrix products, arithmetic and copies ran while one was open for 0% of the time, Pallas kernels for 7%

profile of v4, /device:TPU:0, one launch (start us, length us, event | category | flops | bytes accessed | tf_op | source)
XLA Modules:
  0.0 76.6 jit_solution(14225503516524036964)
XLA Ops:
  0.8 0.7 copy-done.1
  1.5 21.8 %front.1 = (f32[12,32,128,128]{3,2,1,0:T(8,128)S(1)}, f32[2,128,128]{2,1,0:T(8,128)S(1)}, f32[2,128,128]{2,1,0:T(8,128)S(1)}, f32[2,128,128]{2,1,0:T(8,128)S(1)}...) custom-call(f32[4,32,128,128]{3,2,1,0:T(8,128)} %f_ref.1, f32[4,16]{1,0:T(4,128)} %bitcast.15, f32[1,16]{1,0:T(1,128)} %bitcast.16, ...), custom_call_target="tpu_custom_call" | custom-call | tf_op jit(solution)/shard_map/front/pallas_call | solution.py:247
  23.9 0.8 %collective-permute-done.refs_1_.refs_3_ = f32[2,128,128]{2,1,0:T(8,128)S(1)} collective-permute-done((f32[2,128,128]{2,1,0:T(8,128)S(1)}, f32[2,128,128]{2,1,0:T(8,128)S(1)}, u32[]{:S(2)}, u32[]{:S(2)}) %collective-permute-start) | collective-permute-done | bytes 131104 | tf_op jit(solution)/shard_map/ppermute | solution.py:301
  25.3 1.7 %collective-permute-start.1 = (f32[2,128,128]{2,1,0:T(8,128)S(1)}, f32[2,128,128]{2,1,0:T(8,128)S(1)}, u32[]{:S(2)}, u32[]{:S(2)}) collective-permute-start(f32[2,128,128]{2,1,0:T(8,128)S(1)} %combine.10.refs_0_), channel_id=1, source_target_pairs={{0,8},{4,12},{8,0},{12,4},{16,24},{20,28},{24,16},{28,20},{32,40},... | collective-permute-start | bytes 393224 | tf_op jit(solution)/shard_map/ppermute | solution.py:301
  28.1 3.7 %collective-permute-done.1.refs_1_ = f32[2,128,128]{2,1,0:T(8,128)S(1)} collective-permute-done((f32[2,128,128]{2,1,0:T(8,128)S(1)}, f32[2,128,128]{2,1,0:T(8,128)S(1)}, u32[]{:S(2)}, u32[]{:S(2)}) %collective-permute-start.1) | collective-permute-done | bytes 131104 | tf_op jit(solution)/shard_map/ppermute | solution.py:301
  32.3 2.9 %collective-permute-start.2 = (f32[2,128,128]{2,1,0:T(8,128)S(1)}, f32[2,128,128]{2,1,0:T(8,128)S(1)}, u32[]{:S(2)}, u32[]{:S(2)}) collective-permute-start(f32[2,128,128]{2,1,0:T(8,128)S(1)} %get-tuple-element.32.refs_0_), channel_id=1, source_target_pairs={{0,24},{4,28},{8,16},{12,20},{16,8},{20,12},{24,0},{28,4},{32,56},... | collective-permute-start | bytes 393224 | tf_op jit(solution)/shard_map/ppermute | solution.py:301
  35.8 1.4 %collective-permute-start.7 = (f32[2,128,128]{2,1,0:T(8,128)S(1)}, f32[2,128,128]{2,1,0:T(8,128)S(1)}, u32[]{:S(2)}, u32[]{:S(2)}) collective-permute-start(f32[2,128,128]{2,1,0:T(8,128)S(1)} %get-tuple-element.41.refs_0_), channel_id=1, source_target_pairs={{0,24},{4,28},{8,16},{12,20},{16,8},{20,12},{24,0},{28,4},{32,56},... | collective-permute-start | bytes 393224 | tf_op jit(solution)/shard_map/ppermute | solution.py:301
  37.2 2.0 %collective-permute-done.2.refs_1_ = f32[2,128,128]{2,1,0:T(8,128)S(1)} collective-permute-done((f32[2,128,128]{2,1,0:T(8,128)S(1)}, f32[2,128,128]{2,1,0:T(8,128)S(1)}, u32[]{:S(2)}, u32[]{:S(2)}) %collective-permute-start.2) | collective-permute-done | bytes 131104 | tf_op jit(solution)/shard_map/ppermute | solution.py:301
  39.8 1.8 %collective-permute-start.3 = (f32[2,128,128]{2,1,0:T(8,128)S(1)}, f32[2,128,128]{2,1,0:T(8,128)S(1)}, u32[]{:S(2)}, u32[]{:S(2)}) collective-permute-start(f32[2,128,128]{2,1,0:T(8,128)S(1)} %get-tuple-element.34.refs_0_), channel_id=1, source_target_pairs={{0,32},{4,36},{8,40},{12,44},{16,48},{20,52},{24,56},{28,60},{32,0... | collective-permute-start | bytes 393224 | tf_op jit(solution)/shard_map/ppermute | solution.py:301
  42.6 1.7 %collective-permute-start.8 = (f32[2,128,128]{2,1,0:T(8,128)S(1)}, f32[2,128,128]{2,1,0:T(8,128)S(1)}, u32[]{:S(2)}, u32[]{:S(2)}) collective-permute-start(f32[2,128,128]{2,1,0:T(8,128)S(1)} %get-tuple-element.43.refs_0_), channel_id=1, source_target_pairs={{0,32},{4,36},{8,40},{12,44},{16,48},{20,52},{24,56},{28,60},{32,0... | collective-permute-start | bytes 393224 | tf_op jit(solution)/shard_map/ppermute | solution.py:301
  44.3 1.6 %collective-permute-done.3.refs_1_ = f32[2,128,128]{2,1,0:T(8,128)S(1)} collective-permute-done((f32[2,128,128]{2,1,0:T(8,128)S(1)}, f32[2,128,128]{2,1,0:T(8,128)S(1)}, u32[]{:S(2)}, u32[]{:S(2)}) %collective-permute-start.3) | collective-permute-done | bytes 131104 | tf_op jit(solution)/shard_map/ppermute | solution.py:301
  46.4 3.2 %collective-permute-start.4 = (f32[2,128,128]{2,1,0:T(8,128)S(1)}, f32[2,128,128]{2,1,0:T(8,128)S(1)}, u32[]{:S(2)}, u32[]{:S(2)}) collective-permute-start(f32[2,128,128]{2,1,0:T(8,128)S(1)} %get-tuple-element.36), channel_id=1, source_target_pairs={{0,96},{4,100},{8,104},{12,108},{16,112},{20,116},{24,120},{28,124... | collective-permute-start | bytes 393224 | tf_op jit(solution)/shard_map/ppermute | solution.py:301
  50.2 1.2 %collective-permute-start.9 = (f32[2,128,128]{2,1,0:T(8,128)S(1)}, f32[2,128,128]{2,1,0:T(8,128)S(1)}, u32[]{:S(2)}, u32[]{:S(2)}) collective-permute-start(f32[2,128,128]{2,1,0:T(8,128)S(1)} %get-tuple-element.45), channel_id=1, source_target_pairs={{0,96},{4,100},{8,104},{12,108},{16,112},{20,116},{24,120},{28,124... | collective-permute-start | bytes 393224 | tf_op jit(solution)/shard_map/ppermute | solution.py:301
  51.3 1.6 %collective-permute-done.4.refs_0_ = f32[2,128,128]{2,1,0:T(8,128)S(1)} collective-permute-done((f32[2,128,128]{2,1,0:T(8,128)S(1)}, f32[2,128,128]{2,1,0:T(8,128)S(1)}, u32[]{:S(2)}, u32[]{:S(2)}) %collective-permute-start.4) | collective-permute-done | bytes 131104 | tf_op jit(solution)/shard_map/ppermute | solution.py:301
  53.6 2.8 %collective-permute-done.9.refs_0_ = f32[2,128,128]{2,1,0:T(8,128)S(1)} collective-permute-done((f32[2,128,128]{2,1,0:T(8,128)S(1)}, f32[2,128,128]{2,1,0:T(8,128)S(1)}, u32[]{:S(2)}, u32[]{:S(2)}) %collective-permute-start.9) | collective-permute-done | bytes 131104 | tf_op jit(solution)/shard_map/ppermute | solution.py:301
  56.4 0.6 combine.19
  57.1 1.3 %collective-permute-done.11.rest_3_ = f32[2,128,128]{2,1,0:T(8,128)S(1)} collective-permute-done((f32[2,128,128]{2,1,0:T(8,128)S(1)}, f32[2,128,128]{2,1,0:T(8,128)S(1)}, u32[]{:S(2)}, u32[]{:S(2)}) %collective-permute-start.11) | collective-permute-done | bytes 131104 | tf_op jit(solution)/shard_map/ppermute | solution.py:301
  58.4 7.5 %back.1 = (f32[3,32,128,128]{3,2,1,0:T(8,128)}, f32[4,8,128]{2,1,0:T(8,128)S(1)}, f32[4,8,128]{2,1,0:T(8,128)S(1)}, f32[4,8,128]{2,1,0:T(8,128)S(1)}, f32[4,8,128]{2,1,0:T(8,128)S(1)}) custom-call(f32[12,32,128,128]{3,2,1,0:T(8,128)S(1)} %get-tuple-element.29.mid_ref, f32[2,128,128]{2,1,0:T(8,128)S(1)} %get-tuple-element.38.rest_0_, ...), custom_call_target="tpu_custom_call" | custom-call | tf_op jit(solution)/shard_map/back/pallas_call | solution.py:283
  66.0 1.9 %collective-permute-start.12 = (f32[4,8,128]{2,1,0:T(8,128)S(1)}, f32[4,8,128]{2,1,0:T(8,128)S(1)}, u32[]{:S(2)}, u32[]{:S(2)}) collective-permute-start(f32[4,8,128]{2,1,0:T(8,128)S(1)} %get-tuple-element.53), channel_id=1, source_target_pairs={{0,1},{1,2},{2,3},{3,0},{4,5},{5,6},{6,7},{7,4},{8,9},{9,10},{10,1... | collective-permute-start | bytes 49160 | tf_op jit(solution)/shard_map/ppermute | solution.py:378
  67.9 3.6 %collective-permute-start.13 = (f32[4,8,128]{2,1,0:T(8,128)S(1)}, f32[4,8,128]{2,1,0:T(8,128)S(1)}, u32[]{:S(2)}, u32[]{:S(2)}) collective-permute-start(f32[4,8,128]{2,1,0:T(8,128)S(1)} %get-tuple-element.54), channel_id=1, source_target_pairs={{0,2},{1,3},{2,0},{3,1},{4,6},{5,7},{6,4},{7,5},{8,10},{9,11},{10,... | collective-permute-start | bytes 49160 | tf_op jit(solution)/shard_map/ppermute | solution.py:378
  71.5 1.0 %collective-permute-start.14 = (f32[4,8,128]{2,1,0:T(8,128)S(1)}, f32[4,8,128]{2,1,0:T(8,128)S(1)}, u32[]{:S(2)}, u32[]{:S(2)}) collective-permute-start(f32[4,8,128]{2,1,0:T(8,128)S(1)} %get-tuple-element.55), channel_id=1, source_target_pairs={{0,3},{1,0},{2,1},{3,2},{4,7},{5,4},{6,5},{7,6},{8,11},{9,8},{10,9... | collective-permute-start | bytes 49160 | tf_op jit(solution)/shard_map/ppermute | solution.py:378
  72.5 0.9 %collective-permute-done.13.refs_2_ = f32[4,8,128]{2,1,0:T(8,128)S(1)} collective-permute-done((f32[4,8,128]{2,1,0:T(8,128)S(1)}, f32[4,8,128]{2,1,0:T(8,128)S(1)}, u32[]{:S(2)}, u32[]{:S(2)}) %collective-permute-start.13) | collective-permute-done | bytes 16416 | tf_op jit(solution)/shard_map/ppermute | solution.py:378
  73.4 1.9 %collective-permute-done.14.refs_3_ = f32[4,8,128]{2,1,0:T(8,128)S(1)} collective-permute-done((f32[4,8,128]{2,1,0:T(8,128)S(1)}, f32[4,8,128]{2,1,0:T(8,128)S(1)}, u32[]{:S(2)}, u32[]{:S(2)}) %collective-permute-start.14) | collective-permute-done | bytes 16416 | tf_op jit(solution)/shard_map/ppermute | solution.py:378
  75.9 0.7 copy.11
  (27 shorter events, 7.6 us)
Async XLA Ops:
  0.6 57.8 %copy-start = (f32[3,8]{1,0:T(4,128)S(1)}, f32[3,8]{1,0:T(4,128)}, u32[]{:S(2)}) copy-start(f32[3,8]{1,0:T(4,128)} %rest_7_.1) | copy-start | bytes 292
  0.8 0.7 copy-start.1
  23.3 1.4 %collective-permute-start = (f32[2,128,128]{2,1,0:T(8,128)S(1)}, f32[2,128,128]{2,1,0:T(8,128)S(1)}, u32[]{:S(2)}, u32[]{:S(2)}) collective-permute-start(f32[2,128,128]{2,1,0:T(8,128)S(1)} %get-tuple-element.31), channel_id=1, source_target_pairs={{0,4},{4,0},{8,12},{12,8},{16,20},{20,16},{24,28},{28,24},{32,36},... | collective-permute-start | bytes 393224 | tf_op jit(solution)/shard_map/ppermute | solution.py:301
  23.4 3.6 %collective-permute-start.5 = (f32[2,128,128]{2,1,0:T(8,128)S(1)}, f32[2,128,128]{2,1,0:T(8,128)S(1)}, u32[]{:S(2)}, u32[]{:S(2)}) collective-permute-start(f32[2,128,128]{2,1,0:T(8,128)S(1)} %get-tuple-element.40), channel_id=1, source_target_pairs={{0,4},{4,0},{8,12},{12,8},{16,20},{20,16},{24,28},{28,24},{32,36},... | collective-permute-start | bytes 393224 | tf_op jit(solution)/shard_map/ppermute | solution.py:301
  25.3 6.4 %collective-permute-start.1 = (f32[2,128,128]{2,1,0:T(8,128)S(1)}, f32[2,128,128]{2,1,0:T(8,128)S(1)}, u32[]{:S(2)}, u32[]{:S(2)}) collective-permute-start(f32[2,128,128]{2,1,0:T(8,128)S(1)} %combine.10.refs_0_), channel_id=1, source_target_pairs={{0,8},{4,12},{8,0},{12,4},{16,24},{20,28},{24,16},{28,20},{32,40},... | collective-permute-start | bytes 393224 | tf_op jit(solution)/shard_map/ppermute | solution.py:301
  27.5 7.7 %collective-permute-start.6 = (f32[2,128,128]{2,1,0:T(8,128)S(1)}, f32[2,128,128]{2,1,0:T(8,128)S(1)}, u32[]{:S(2)}, u32[]{:S(2)}) collective-permute-start(f32[2,128,128]{2,1,0:T(8,128)S(1)} %combine.15.refs_0_), channel_id=1, source_target_pairs={{0,8},{4,12},{8,0},{12,4},{16,24},{20,28},{24,16},{28,20},{32,40},... | collective-permute-start | bytes 393224 | tf_op jit(solution)/shard_map/ppermute | solution.py:301
  32.3 6.9 %collective-permute-start.2 = (f32[2,128,128]{2,1,0:T(8,128)S(1)}, f32[2,128,128]{2,1,0:T(8,128)S(1)}, u32[]{:S(2)}, u32[]{:S(2)}) collective-permute-start(f32[2,128,128]{2,1,0:T(8,128)S(1)} %get-tuple-element.32.refs_0_), channel_id=1, source_target_pairs={{0,24},{4,28},{8,16},{12,20},{16,8},{20,12},{24,0},{28,4},{32,56},... | collective-permute-start | bytes 393224 | tf_op jit(solution)/shard_map/ppermute | solution.py:301
  35.8 6.3 %collective-permute-start.7 = (f32[2,128,128]{2,1,0:T(8,128)S(1)}, f32[2,128,128]{2,1,0:T(8,128)S(1)}, u32[]{:S(2)}, u32[]{:S(2)}) collective-permute-start(f32[2,128,128]{2,1,0:T(8,128)S(1)} %get-tuple-element.41.refs_0_), channel_id=1, source_target_pairs={{0,24},{4,28},{8,16},{12,20},{16,8},{20,12},{24,0},{28,4},{32,56},... | collective-permute-start | bytes 393224 | tf_op jit(solution)/shard_map/ppermute | solution.py:301
  39.8 6.0 %collective-permute-start.3 = (f32[2,128,128]{2,1,0:T(8,128)S(1)}, f32[2,128,128]{2,1,0:T(8,128)S(1)}, u32[]{:S(2)}, u32[]{:S(2)}) collective-permute-start(f32[2,128,128]{2,1,0:T(8,128)S(1)} %get-tuple-element.34.refs_0_), channel_id=1, source_target_pairs={{0,32},{4,36},{8,40},{12,44},{16,48},{20,52},{24,56},{28,60},{32,0... | collective-permute-start | bytes 393224 | tf_op jit(solution)/shard_map/ppermute | solution.py:301
  42.6 7.0 %collective-permute-start.8 = (f32[2,128,128]{2,1,0:T(8,128)S(1)}, f32[2,128,128]{2,1,0:T(8,128)S(1)}, u32[]{:S(2)}, u32[]{:S(2)}) collective-permute-start(f32[2,128,128]{2,1,0:T(8,128)S(1)} %get-tuple-element.43.refs_0_), channel_id=1, source_target_pairs={{0,32},{4,36},{8,40},{12,44},{16,48},{20,52},{24,56},{28,60},{32,0... | collective-permute-start | bytes 393224 | tf_op jit(solution)/shard_map/ppermute | solution.py:301
  46.4 6.5 %collective-permute-start.4 = (f32[2,128,128]{2,1,0:T(8,128)S(1)}, f32[2,128,128]{2,1,0:T(8,128)S(1)}, u32[]{:S(2)}, u32[]{:S(2)}) collective-permute-start(f32[2,128,128]{2,1,0:T(8,128)S(1)} %get-tuple-element.36), channel_id=1, source_target_pairs={{0,96},{4,100},{8,104},{12,108},{16,112},{20,116},{24,120},{28,124... | collective-permute-start | bytes 393224 | tf_op jit(solution)/shard_map/ppermute | solution.py:301
  50.2 6.3 %collective-permute-start.9 = (f32[2,128,128]{2,1,0:T(8,128)S(1)}, f32[2,128,128]{2,1,0:T(8,128)S(1)}, u32[]{:S(2)}, u32[]{:S(2)}) collective-permute-start(f32[2,128,128]{2,1,0:T(8,128)S(1)} %get-tuple-element.45), channel_id=1, source_target_pairs={{0,96},{4,100},{8,104},{12,108},{16,112},{20,116},{24,120},{28,124... | collective-permute-start | bytes 393224 | tf_op jit(solution)/shard_map/ppermute | solution.py:301
  53.5 3.6 %collective-permute-start.10 = (f32[2,128,128]{2,1,0:T(8,128)S(1)}, f32[2,128,128]{2,1,0:T(8,128)S(1)}, u32[]{:S(2)}, u32[]{:S(2)}) collective-permute-start(f32[2,128,128]{2,1,0:T(8,128)S(1)} %get-tuple-element.48), channel_id=1, source_target_pairs={{0,4},{4,0},{8,12},{12,8},{16,20},{20,16},{24,28},{28,24},{32,36},... | collective-permute-start | bytes 393224 | tf_op jit(solution)/shard_map/ppermute | solution.py:301
  57.0 1.4 %collective-permute-start.11 = (f32[2,128,128]{2,1,0:T(8,128)S(1)}, f32[2,128,128]{2,1,0:T(8,128)S(1)}, u32[]{:S(2)}, u32[]{:S(2)}) collective-permute-start(f32[2,128,128]{2,1,0:T(8,128)S(1)} %get-tuple-element.49), channel_id=1, source_target_pairs={{0,4},{4,0},{8,12},{12,8},{16,20},{20,16},{24,28},{28,24},{32,36},... | collective-permute-start | bytes 393224 | tf_op jit(solution)/shard_map/ppermute | solution.py:301
  66.0 6.5 %collective-permute-start.12 = (f32[4,8,128]{2,1,0:T(8,128)S(1)}, f32[4,8,128]{2,1,0:T(8,128)S(1)}, u32[]{:S(2)}, u32[]{:S(2)}) collective-permute-start(f32[4,8,128]{2,1,0:T(8,128)S(1)} %get-tuple-element.53), channel_id=1, source_target_pairs={{0,1},{1,2},{2,3},{3,0},{4,5},{5,6},{6,7},{7,4},{8,9},{9,10},{10,1... | collective-permute-start | bytes 49160 | tf_op jit(solution)/shard_map/ppermute | solution.py:378
  67.9 5.5 %collective-permute-start.13 = (f32[4,8,128]{2,1,0:T(8,128)S(1)}, f32[4,8,128]{2,1,0:T(8,128)S(1)}, u32[]{:S(2)}, u32[]{:S(2)}) collective-permute-start(f32[4,8,128]{2,1,0:T(8,128)S(1)} %get-tuple-element.54), channel_id=1, source_target_pairs={{0,2},{1,3},{2,0},{3,1},{4,6},{5,7},{6,4},{7,5},{8,10},{9,11},{10,... | collective-permute-start | bytes 49160 | tf_op jit(solution)/shard_map/ppermute | solution.py:378
  71.5 3.7 %collective-permute-start.14 = (f32[4,8,128]{2,1,0:T(8,128)S(1)}, f32[4,8,128]{2,1,0:T(8,128)S(1)}, u32[]{:S(2)}, u32[]{:S(2)}) collective-permute-start(f32[4,8,128]{2,1,0:T(8,128)S(1)} %get-tuple-element.55), channel_id=1, source_target_pairs={{0,3},{1,0},{2,1},{3,2},{4,7},{5,4},{6,5},{7,6},{8,11},{9,8},{10,9... | collective-permute-start | bytes 49160 | tf_op jit(solution)/shard_map/ppermute | solution.py:378

commit v5 on v4

--- a/solution.py
+++ b/solution.py
@@ -83,12 +83,14 @@
                  mid_ref, *rest):
     cells_x = f_ref.shape[1]
     send_refs, keep_refs = rest[:PIECES], rest[PIECES : 2 * PIECES]
-    dep_ref, first_ref, second_ref, tri_ref = rest[2 * PIECES :]
+    dep_ref, flag_ref, first_ref, second_ref, tri_ref = rest[2 * PIECES :]
     step = pl.program_id(0)
     core = core_ref[0]
 
     @pl.when(step == 0)
     def _():
+        for i in range(6):
+            flag_ref[i] = jnp.full((8, 128), core_ref[i], jnp.int32).astype(F32)
         high, low, bias = build_first(win_ref[...].T, bin_ref[...])
         first_ref[:, 0:64] = high
         first_ref[:, 64:128] = high
@@ -257,11 +259,13 @@
             whole,
             *[pl.BlockSpec((EACH, SLAB, cells_z), lambda i: (0, i, 0))] * (2 * PIECES),
             pl.BlockSpec((1, 8, 128), lambda i: (i // each, 0, 0)),
+            whole,
         ],
         out_shape=[
             pltpu.MemorySpace.VMEM((OUTS, cells_x, rows_y, cells_z), F32),
             *[jax.ShapeDtypeStruct((EACH, rows_y, cells_z), F32)] * (2 * PIECES),
             jax.ShapeDtypeStruct((rows_y // SLAB // each, 8, 128), F32),
+            jax.ShapeDtypeStruct((6, 8, 128), F32),
         ],
         scratch_shapes=[
             pltpu.VMEM((SLAB * UNITS, 208), BF16),
@@ -309,8 +313,8 @@
     whole = pl.BlockSpec(memory_space=pltpu.VMEM)
     shape = arrays[0].shape
 
-    def kernel(place_ref, *refs):
-        where = [place_ref[i] for i in range(6)]
+    def kernel(flag_ref, *refs):
+        where = [flag_ref[i, 0:1] for i in range(5)]
         for band in range(shape[0]):
             values = [ref[band] for ref in refs[: len(arrays)]]
             for ref, value in zip(refs[len(arrays) :], body(where, *values), strict=True):
@@ -318,7 +322,7 @@
 
     return pl.pallas_call(
         kernel,
-        in_specs=[pl.BlockSpec(memory_space=pltpu.SMEM)] + [whole] * len(arrays),
+        in_specs=[whole] * (1 + len(arrays)),
         out_specs=[whole] * outputs,
         out_shape=[jax.ShapeDtypeStruct(shape, F32)] * outputs,
         compiler_params=pltpu.CompilerParams(vmem_limit_bytes=4 << 20),
@@ -341,11 +345,11 @@
         other = swap(total, "gx", partner)
 
         def merge(where, total, other, before=0.0):
-            return [total + other, before + jnp.where(where[1 + stage] == 1, other, 0.0)]
+            return [total + other, before + other * where[1 + stage]]
 
         def last(where, other, before, keep, got):
-            before = before + jnp.where(where[1 + stage] == 1, other, 0.0)
-            return [before + jnp.where(where[0] == 0, 0.0, got), before + jnp.where(where[0] == 0, keep, 0.0)]
+            before = before + other * where[1 + stage]
+            return [before + got * where[0], before + keep * (1.0 - where[0])]
 
         if stage < 3:
             total, before = small_kernel(merge, [total, other] + ([before] if stage else []), place, 2)
@@ -354,10 +358,11 @@
     return mine, swap(theirs, "gx", lambda i: i ^ 1)
 
 
-def compose_kernel(place_ref, *refs):
+def compose_kernel(flag_ref, *refs):
     pieces, out_ref = refs[:-1], refs[-1]
     ndev = len(pieces)
-    origin = [(place_ref[5] - apart + ndev) % ndev for apart in range(ndev)]
+    origin = [flag_ref[5] - apart for apart in range(ndev)]
+    origin = [jnp.where(value < 0.0, value + ndev, value) for value in origin]
     depths = [piece[3] for piece in pieces]
     totals = [jnp.zeros_like(depths[0])] * 3
     for i in range(ndev):
@@ -372,7 +377,7 @@
     out_ref[3] = 1.0 - jnp.exp(-sum(depths[1:], depths[0]))
 
 
-def composite(pieces, place, cells_x):
+def composite(pieces, flags, cells_x):
     ndev = len(pieces)
     held = [
         lax.ppermute(piece, "gz", [(i, (i + apart) % ndev) for i in range(ndev)]) if apart else piece
@@ -381,12 +386,12 @@
     whole = pl.BlockSpec(memory_space=pltpu.VMEM)
     image = pl.pallas_call(
         compose_kernel,
-        in_specs=[pl.BlockSpec(memory_space=pltpu.SMEM)] + [whole] * ndev,
+        in_specs=[whole] * (1 + ndev),
         out_specs=whole,
         out_shape=jax.ShapeDtypeStruct(pieces[0].shape, F32),
         compiler_params=pltpu.CompilerParams(vmem_limit_bytes=4 << 20),
         name="compose",
-    )(place, *held)
+    )(flags, *held)
     image = image.reshape(4, 8, 128 // cells_x, cells_x)
     return image.transpose(0, 3, 2, 1).reshape(4, cells_x, -1)
 
@@ -399,12 +404,12 @@
     me = lax.axis_index("gx")
     place = jnp.stack([me % 2, me // 2 % 2, me // 4 % 2, me // 8 % 2, me // 16 % 2,
                        lax.axis_index("gz")]).astype(jnp.int32)
-    mid, *sums, dep = front(
+    mid, *sums, dep, flags = front(
         features, w_in, b_in, w_out, b_out, band_depth, place, total_x, total_z, 0, rows_y)
-    scanned = [scan_x(sums[i], sums[PIECES + i], place) for i in range(PIECES)]
+    scanned = [scan_x(sums[i], sums[PIECES + i], flags) for i in range(PIECES)]
     incoming = [mine for mine, _ in scanned] + [theirs for _, theirs in scanned]
     light, *pieces = back(mid, incoming, dep, band_depth, place, band_mix, total_x, lax.axis_size("gz"))
-    return light, composite(pieces, place, cells_x)
+    return light, composite(pieces, flags, cells_x)
 
 
 def solution(mesh):

time: 77.3 us -> 73.5 us (0.951)
  Pallas kernels: 35.6 us -> 29.6 us
  waiting for transfers between devices: 16.9 us -> 18.5 us
    pallas_call x11, Pallas kernels: 6.24 us -> 0.29 us  [the longest x10 0.27 us: small_kernel(): pl.pallas_call(kernel, in_specs=[whole] * (1 + len(arrays)), out_specs=[w...]
    ppermute x12, waiting for transfers between devices: 14.2 us -> 15.7 us  [swap(): lax.ppermute(value, axis, [(i, partner(i)) for i in range(lax.axis_size(a...]
  transfers between devices with their start and end apart: 15 -> 15, of which waited for: 10 -> 10; matrix products, arithmetic and copies ran while one was open for 0% -> 0% of each run, Pallas kernels for 7% -> 0%
where the time goes in v5:
time: 73.5 us; the launch traced here: 72.8 us
  Pallas kernels  29.6 us (40%)
  starting transfers between devices  22.3 us (30%)
  waiting for transfers between devices  18.5 us (25%)
  local copies, waits for them, and re-layouts  1.56 us (2%)
  between operations  0.84 us (1%)
    pallas_call x1, Pallas kernels, front(): pl.pallas_call(functools.partial(front_kernel, total_x, total_z, 2, 2), g...  21.8 us
    ppermute x12, starting transfers between devices, swap(): lax.ppermute(value, axis, [(i, partner(i)) for i in range(lax.axis_size(a...  15.8 us
    ppermute x12, waiting for transfers between devices, swap(): lax.ppermute(value, axis, [(i, partner(i)) for i in range(lax.axis_size(a...  15.7 us
    pallas_call x1, Pallas kernels, back(): pl.pallas_call(functools.partial(back_kernel, total_x, cells_x), grid=(sl...  7.53 us
    ppermute x3, starting transfers between devices, composite(): lax.ppermute(piece, 'gz', [(i, (i + apart) % ndev) for i in range(ndev)])  6.51 us
    ppermute x3, waiting for transfers between devices, composite(): lax.ppermute(piece, 'gz', [(i, (i + apart) % ndev) for i in range(ndev)])  2.73 us
  transfers between devices with their start and end apart: 15, of which 10 were waited for; matrix products, arithmetic and copies ran while one was open for 0% of the time, Pallas kernels for 0%

profile of v5, /device:TPU:0, one launch (start us, length us, event | category | flops | bytes accessed | tf_op | source)
XLA Modules:
  0.0 72.8 jit_solution(8999439543793181311)
XLA Ops:
  0.8 0.7 copy-done.1
  1.5 21.8 %front.1 = (f32[12,32,128,128]{3,2,1,0:T(8,128)S(1)}, f32[2,128,128]{2,1,0:T(8,128)S(1)}, f32[2,128,128]{2,1,0:T(8,128)S(1)}, f32[2,128,128]{2,1,0:T(8,128)S(1)}...) custom-call(f32[4,32,128,128]{3,2,1,0:T(8,128)} %f_ref.1, f32[4,16]{1,0:T(4,128)} %bitcast.15, ...), custom_call_target="tpu_custom_call" | custom-call | tf_op jit(solution)/shard_map/front/pallas_call | solution.py:249
  23.9 0.8 %collective-permute-done.refs_1_.refs_3_ = f32[2,128,128]{2,1,0:T(8,128)S(1)} collective-permute-done((f32[2,128,128]{2,1,0:T(8,128)S(1)}, f32[2,128,128]{2,1,0:T(8,128)S(1)}, u32[]{:S(2)}, u32[]{:S(2)}) %collective-permute-start) | collective-permute-done | bytes 131104 | tf_op jit(solution)/shard_map/ppermute | solution.py:305
  24.8 1.7 %collective-permute-start.1 = (f32[2,128,128]{2,1,0:T(8,128)S(1)}, f32[2,128,128]{2,1,0:T(8,128)S(1)}, u32[]{:S(2)}, u32[]{:S(2)}) collective-permute-start(f32[2,128,128]{2,1,0:T(8,128)S(1)} %combine.10.refs_0_), channel_id=1, source_target_pairs={{0,8},{4,12},{8,0},{12,4},{16,24},{20,28},{24,16},{28,20},{32,40},... | collective-permute-start | bytes 393224 | tf_op jit(solution)/shard_map/ppermute | solution.py:305
  26.5 0.5 collective-permute-start.6
  27.0 4.2 %collective-permute-done.1.refs_1_ = f32[2,128,128]{2,1,0:T(8,128)S(1)} collective-permute-done((f32[2,128,128]{2,1,0:T(8,128)S(1)}, f32[2,128,128]{2,1,0:T(8,128)S(1)}, u32[]{:S(2)}, u32[]{:S(2)}) %collective-permute-start.1) | collective-permute-done | bytes 131104 | tf_op jit(solution)/shard_map/ppermute | solution.py:305
  31.2 2.9 %collective-permute-start.2 = (f32[2,128,128]{2,1,0:T(8,128)S(1)}, f32[2,128,128]{2,1,0:T(8,128)S(1)}, u32[]{:S(2)}, u32[]{:S(2)}) collective-permute-start(f32[2,128,128]{2,1,0:T(8,128)S(1)} %get-tuple-element.34.refs_0_), channel_id=1, source_target_pairs={{0,24},{4,28},{8,16},{12,20},{16,8},{20,12},{24,0},{28,4},{32,56},... | collective-permute-start | bytes 393224 | tf_op jit(solution)/shard_map/ppermute | solution.py:305
  34.2 2.0 %collective-permute-start.7 = (f32[2,128,128]{2,1,0:T(8,128)S(1)}, f32[2,128,128]{2,1,0:T(8,128)S(1)}, u32[]{:S(2)}, u32[]{:S(2)}) collective-permute-start(f32[2,128,128]{2,1,0:T(8,128)S(1)} %get-tuple-element.43.refs_0_), channel_id=1, source_target_pairs={{0,24},{4,28},{8,16},{12,20},{16,8},{20,12},{24,0},{28,4},{32,56},... | collective-permute-start | bytes 393224 | tf_op jit(solution)/shard_map/ppermute | solution.py:305
  36.2 2.4 %collective-permute-done.2.refs_1_ = f32[2,128,128]{2,1,0:T(8,128)S(1)} collective-permute-done((f32[2,128,128]{2,1,0:T(8,128)S(1)}, f32[2,128,128]{2,1,0:T(8,128)S(1)}, u32[]{:S(2)}, u32[]{:S(2)}) %collective-permute-start.2) | collective-permute-done | bytes 131104 | tf_op jit(solution)/shard_map/ppermute | solution.py:305
  38.6 1.7 %collective-permute-start.3 = (f32[2,128,128]{2,1,0:T(8,128)S(1)}, f32[2,128,128]{2,1,0:T(8,128)S(1)}, u32[]{:S(2)}, u32[]{:S(2)}) collective-permute-start(f32[2,128,128]{2,1,0:T(8,128)S(1)} %get-tuple-element.36.refs_0_), channel_id=1, source_target_pairs={{0,32},{4,36},{8,40},{12,44},{16,48},{20,52},{24,56},{28,60},{32,0... | collective-permute-start | bytes 393224 | tf_op jit(solution)/shard_map/ppermute | solution.py:305
  40.5 1.6 %collective-permute-start.8 = (f32[2,128,128]{2,1,0:T(8,128)S(1)}, f32[2,128,128]{2,1,0:T(8,128)S(1)}, u32[]{:S(2)}, u32[]{:S(2)}) collective-permute-start(f32[2,128,128]{2,1,0:T(8,128)S(1)} %get-tuple-element.45.refs_0_), channel_id=1, source_target_pairs={{0,32},{4,36},{8,40},{12,44},{16,48},{20,52},{24,56},{28,60},{32,0... | collective-permute-start | bytes 393224 | tf_op jit(solution)/shard_map/ppermute | solution.py:305
  42.1 2.1 %collective-permute-done.3.refs_1_ = f32[2,128,128]{2,1,0:T(8,128)S(1)} collective-permute-done((f32[2,128,128]{2,1,0:T(8,128)S(1)}, f32[2,128,128]{2,1,0:T(8,128)S(1)}, u32[]{:S(2)}, u32[]{:S(2)}) %collective-permute-start.3) | collective-permute-done | bytes 131104 | tf_op jit(solution)/shard_map/ppermute | solution.py:305
  44.3 3.2 %collective-permute-start.4 = (f32[2,128,128]{2,1,0:T(8,128)S(1)}, f32[2,128,128]{2,1,0:T(8,128)S(1)}, u32[]{:S(2)}, u32[]{:S(2)}) collective-permute-start(f32[2,128,128]{2,1,0:T(8,128)S(1)} %get-tuple-element.38), channel_id=1, source_target_pairs={{0,96},{4,100},{8,104},{12,108},{16,112},{20,116},{24,120},{28,124... | collective-permute-start | bytes 393224 | tf_op jit(solution)/shard_map/ppermute | solution.py:305
  47.5 1.4 %collective-permute-start.9 = (f32[2,128,128]{2,1,0:T(8,128)S(1)}, f32[2,128,128]{2,1,0:T(8,128)S(1)}, u32[]{:S(2)}, u32[]{:S(2)}) collective-permute-start(f32[2,128,128]{2,1,0:T(8,128)S(1)} %get-tuple-element.47), channel_id=1, source_target_pairs={{0,96},{4,100},{8,104},{12,108},{16,112},{20,116},{24,120},{28,124... | collective-permute-start | bytes 393224 | tf_op jit(solution)/shard_map/ppermute | solution.py:305
  48.8 1.7 %collective-permute-done.4.refs_0_ = f32[2,128,128]{2,1,0:T(8,128)S(1)} collective-permute-done((f32[2,128,128]{2,1,0:T(8,128)S(1)}, f32[2,128,128]{2,1,0:T(8,128)S(1)}, u32[]{:S(2)}, u32[]{:S(2)}) %collective-permute-start.4) | collective-permute-done | bytes 131104 | tf_op jit(solution)/shard_map/ppermute | solution.py:305
  50.7 3.1 %collective-permute-done.9.refs_0_ = f32[2,128,128]{2,1,0:T(8,128)S(1)} collective-permute-done((f32[2,128,128]{2,1,0:T(8,128)S(1)}, f32[2,128,128]{2,1,0:T(8,128)S(1)}, u32[]{:S(2)}, u32[]{:S(2)}) %collective-permute-start.9) | collective-permute-done | bytes 131104 | tf_op jit(solution)/shard_map/ppermute | solution.py:305
  53.9 1.3 %collective-permute-done.11.rest_3_ = f32[2,128,128]{2,1,0:T(8,128)S(1)} collective-permute-done((f32[2,128,128]{2,1,0:T(8,128)S(1)}, f32[2,128,128]{2,1,0:T(8,128)S(1)}, u32[]{:S(2)}, u32[]{:S(2)}) %collective-permute-start.11) | collective-permute-done | bytes 131104 | tf_op jit(solution)/shard_map/ppermute | solution.py:305
  55.2 7.5 %back.1 = (f32[3,32,128,128]{3,2,1,0:T(8,128)}, f32[4,8,128]{2,1,0:T(8,128)S(1)}, f32[4,8,128]{2,1,0:T(8,128)S(1)}, f32[4,8,128]{2,1,0:T(8,128)S(1)}, f32[4,8,128]{2,1,0:T(8,128)S(1)}) custom-call(f32[12,32,128,128]{3,2,1,0:T(8,128)S(1)} %get-tuple-element.30.mid_ref, f32[2,128,128]{2,1,0:T(8,128)S(1)} %get-tuple-element.40.rest_0_, ...), custom_call_target="tpu_custom_call" | custom-call | tf_op jit(solution)/shard_map/back/pallas_call | solution.py:287
  62.7 1.9 %collective-permute-start.12 = (f32[4,8,128]{2,1,0:T(8,128)S(1)}, f32[4,8,128]{2,1,0:T(8,128)S(1)}, u32[]{:S(2)}, u32[]{:S(2)}) collective-permute-start(f32[4,8,128]{2,1,0:T(8,128)S(1)} %get-tuple-element.55), channel_id=1, source_target_pairs={{0,1},{1,2},{2,3},{3,0},{4,5},{5,6},{6,7},{7,4},{8,9},{9,10},{10,1... | collective-permute-start | bytes 49160 | tf_op jit(solution)/shard_map/ppermute | solution.py:383
  64.6 3.6 %collective-permute-start.13 = (f32[4,8,128]{2,1,0:T(8,128)S(1)}, f32[4,8,128]{2,1,0:T(8,128)S(1)}, u32[]{:S(2)}, u32[]{:S(2)}) collective-permute-start(f32[4,8,128]{2,1,0:T(8,128)S(1)} %get-tuple-element.56), channel_id=1, source_target_pairs={{0,2},{1,3},{2,0},{3,1},{4,6},{5,7},{6,4},{7,5},{8,10},{9,11},{10,... | collective-permute-start | bytes 49160 | tf_op jit(solution)/shard_map/ppermute | solution.py:383
  68.2 1.0 %collective-permute-start.14 = (f32[4,8,128]{2,1,0:T(8,128)S(1)}, f32[4,8,128]{2,1,0:T(8,128)S(1)}, u32[]{:S(2)}, u32[]{:S(2)}) collective-permute-start(f32[4,8,128]{2,1,0:T(8,128)S(1)} %get-tuple-element.57), channel_id=1, source_target_pairs={{0,3},{1,0},{2,1},{3,2},{4,7},{5,4},{6,5},{7,6},{8,11},{9,8},{10,9... | collective-permute-start | bytes 49160 | tf_op jit(solution)/shard_map/ppermute | solution.py:383
  69.2 0.9 %collective-permute-done.13.refs_2_ = f32[4,8,128]{2,1,0:T(8,128)S(1)} collective-permute-done((f32[4,8,128]{2,1,0:T(8,128)S(1)}, f32[4,8,128]{2,1,0:T(8,128)S(1)}, u32[]{:S(2)}, u32[]{:S(2)}) %collective-permute-start.13) | collective-permute-done | bytes 16416 | tf_op jit(solution)/shard_map/ppermute | solution.py:383
  70.1 1.9 %collective-permute-done.14.refs_3_ = f32[4,8,128]{2,1,0:T(8,128)S(1)} collective-permute-done((f32[4,8,128]{2,1,0:T(8,128)S(1)}, f32[4,8,128]{2,1,0:T(8,128)S(1)}, u32[]{:S(2)}, u32[]{:S(2)}) %collective-permute-start.14) | collective-permute-done | bytes 16416 | tf_op jit(solution)/shard_map/ppermute | solution.py:383
  72.1 0.7 copy.11
  (27 shorter events, 1.3 us)
Async XLA Ops:
  0.6 54.6 %copy-start = (f32[3,8]{1,0:T(4,128)S(1)}, f32[3,8]{1,0:T(4,128)}, u32[]{:S(2)}) copy-start(f32[3,8]{1,0:T(4,128)} %rest_7_.1) | copy-start | bytes 292
  0.8 0.7 copy-start.1
  23.3 1.4 %collective-permute-start = (f32[2,128,128]{2,1,0:T(8,128)S(1)}, f32[2,128,128]{2,1,0:T(8,128)S(1)}, u32[]{:S(2)}, u32[]{:S(2)}) collective-permute-start(f32[2,128,128]{2,1,0:T(8,128)S(1)} %get-tuple-element.33), channel_id=1, source_target_pairs={{0,4},{4,0},{8,12},{12,8},{16,20},{20,16},{24,28},{28,24},{32,36},... | collective-permute-start | bytes 393224 | tf_op jit(solution)/shard_map/ppermute | solution.py:305
  23.4 3.0 %collective-permute-start.5 = (f32[2,128,128]{2,1,0:T(8,128)S(1)}, f32[2,128,128]{2,1,0:T(8,128)S(1)}, u32[]{:S(2)}, u32[]{:S(2)}) collective-permute-start(f32[2,128,128]{2,1,0:T(8,128)S(1)} %get-tuple-element.42), channel_id=1, source_target_pairs={{0,4},{4,0},{8,12},{12,8},{16,20},{20,16},{24,28},{28,24},{32,36},... | collective-permute-start | bytes 393224 | tf_op jit(solution)/shard_map/ppermute | solution.py:305
  24.8 6.4 %collective-permute-start.1 = (f32[2,128,128]{2,1,0:T(8,128)S(1)}, f32[2,128,128]{2,1,0:T(8,128)S(1)}, u32[]{:S(2)}, u32[]{:S(2)}) collective-permute-start(f32[2,128,128]{2,1,0:T(8,128)S(1)} %combine.10.refs_0_), channel_id=1, source_target_pairs={{0,8},{4,12},{8,0},{12,4},{16,24},{20,28},{24,16},{28,20},{32,40},... | collective-permute-start | bytes 393224 | tf_op jit(solution)/shard_map/ppermute | solution.py:305
  26.5 7.7 %collective-permute-start.6 = (f32[2,128,128]{2,1,0:T(8,128)S(1)}, f32[2,128,128]{2,1,0:T(8,128)S(1)}, u32[]{:S(2)}, u32[]{:S(2)}) collective-permute-start(f32[2,128,128]{2,1,0:T(8,128)S(1)} %combine.15.refs_0_), channel_id=1, source_target_pairs={{0,8},{4,12},{8,0},{12,4},{16,24},{20,28},{24,16},{28,20},{32,40},... | collective-permute-start | bytes 393224 | tf_op jit(solution)/shard_map/ppermute | solution.py:305
  31.2 7.4 %collective-permute-start.2 = (f32[2,128,128]{2,1,0:T(8,128)S(1)}, f32[2,128,128]{2,1,0:T(8,128)S(1)}, u32[]{:S(2)}, u32[]{:S(2)}) collective-permute-start(f32[2,128,128]{2,1,0:T(8,128)S(1)} %get-tuple-element.34.refs_0_), channel_id=1, source_target_pairs={{0,24},{4,28},{8,16},{12,20},{16,8},{20,12},{24,0},{28,4},{32,56},... | collective-permute-start | bytes 393224 | tf_op jit(solution)/shard_map/ppermute | solution.py:305
  34.2 6.3 %collective-permute-start.7 = (f32[2,128,128]{2,1,0:T(8,128)S(1)}, f32[2,128,128]{2,1,0:T(8,128)S(1)}, u32[]{:S(2)}, u32[]{:S(2)}) collective-permute-start(f32[2,128,128]{2,1,0:T(8,128)S(1)} %get-tuple-element.43.refs_0_), channel_id=1, source_target_pairs={{0,24},{4,28},{8,16},{12,20},{16,8},{20,12},{24,0},{28,4},{32,56},... | collective-permute-start | bytes 393224 | tf_op jit(solution)/shard_map/ppermute | solution.py:305
  38.6 5.6 %collective-permute-start.3 = (f32[2,128,128]{2,1,0:T(8,128)S(1)}, f32[2,128,128]{2,1,0:T(8,128)S(1)}, u32[]{:S(2)}, u32[]{:S(2)}) collective-permute-start(f32[2,128,128]{2,1,0:T(8,128)S(1)} %get-tuple-element.36.refs_0_), channel_id=1, source_target_pairs={{0,32},{4,36},{8,40},{12,44},{16,48},{20,52},{24,56},{28,60},{32,0... | collective-permute-start | bytes 393224 | tf_op jit(solution)/shard_map/ppermute | solution.py:305
  40.5 7.0 %collective-permute-start.8 = (f32[2,128,128]{2,1,0:T(8,128)S(1)}, f32[2,128,128]{2,1,0:T(8,128)S(1)}, u32[]{:S(2)}, u32[]{:S(2)}) collective-permute-start(f32[2,128,128]{2,1,0:T(8,128)S(1)} %get-tuple-element.45.refs_0_), channel_id=1, source_target_pairs={{0,32},{4,36},{8,40},{12,44},{16,48},{20,52},{24,56},{28,60},{32,0... | collective-permute-start | bytes 393224 | tf_op jit(solution)/shard_map/ppermute | solution.py:305
  44.3 6.3 %collective-permute-start.4 = (f32[2,128,128]{2,1,0:T(8,128)S(1)}, f32[2,128,128]{2,1,0:T(8,128)S(1)}, u32[]{:S(2)}, u32[]{:S(2)}) collective-permute-start(f32[2,128,128]{2,1,0:T(8,128)S(1)} %get-tuple-element.38), channel_id=1, source_target_pairs={{0,96},{4,100},{8,104},{12,108},{16,112},{20,116},{24,120},{28,124... | collective-permute-start | bytes 393224 | tf_op jit(solution)/shard_map/ppermute | solution.py:305
  47.5 6.3 %collective-permute-start.9 = (f32[2,128,128]{2,1,0:T(8,128)S(1)}, f32[2,128,128]{2,1,0:T(8,128)S(1)}, u32[]{:S(2)}, u32[]{:S(2)}) collective-permute-start(f32[2,128,128]{2,1,0:T(8,128)S(1)} %get-tuple-element.47), channel_id=1, source_target_pairs={{0,96},{4,100},{8,104},{12,108},{16,112},{20,116},{24,120},{28,124... | collective-permute-start | bytes 393224 | tf_op jit(solution)/shard_map/ppermute | solution.py:305
  50.6 3.3 %collective-permute-start.10 = (f32[2,128,128]{2,1,0:T(8,128)S(1)}, f32[2,128,128]{2,1,0:T(8,128)S(1)}, u32[]{:S(2)}, u32[]{:S(2)}) collective-permute-start(f32[2,128,128]{2,1,0:T(8,128)S(1)} %get-tuple-element.50), channel_id=1, source_target_pairs={{0,4},{4,0},{8,12},{12,8},{16,20},{20,16},{24,28},{28,24},{32,36},... | collective-permute-start | bytes 393224 | tf_op jit(solution)/shard_map/ppermute | solution.py:305
  53.8 1.4 %collective-permute-start.11 = (f32[2,128,128]{2,1,0:T(8,128)S(1)}, f32[2,128,128]{2,1,0:T(8,128)S(1)}, u32[]{:S(2)}, u32[]{:S(2)}) collective-permute-start(f32[2,128,128]{2,1,0:T(8,128)S(1)} %get-tuple-element.51), channel_id=1, source_target_pairs={{0,4},{4,0},{8,12},{12,8},{16,20},{20,16},{24,28},{28,24},{32,36},... | collective-permute-start | bytes 393224 | tf_op jit(solution)/shard_map/ppermute | solution.py:305
  62.7 6.5 %collective-permute-start.12 = (f32[4,8,128]{2,1,0:T(8,128)S(1)}, f32[4,8,128]{2,1,0:T(8,128)S(1)}, u32[]{:S(2)}, u32[]{:S(2)}) collective-permute-start(f32[4,8,128]{2,1,0:T(8,128)S(1)} %get-tuple-element.55), channel_id=1, source_target_pairs={{0,1},{1,2},{2,3},{3,0},{4,5},{5,6},{6,7},{7,4},{8,9},{9,10},{10,1... | collective-permute-start | bytes 49160 | tf_op jit(solution)/shard_map/ppermute | solution.py:383
  64.6 5.5 %collective-permute-start.13 = (f32[4,8,128]{2,1,0:T(8,128)S(1)}, f32[4,8,128]{2,1,0:T(8,128)S(1)}, u32[]{:S(2)}, u32[]{:S(2)}) collective-permute-start(f32[4,8,128]{2,1,0:T(8,128)S(1)} %get-tuple-element.56), channel_id=1, source_target_pairs={{0,2},{1,3},{2,0},{3,1},{4,6},{5,7},{6,4},{7,5},{8,10},{9,11},{10,... | collective-permute-start | bytes 49160 | tf_op jit(solution)/shard_map/ppermute | solution.py:383
  68.2 3.7 %collective-permute-start.14 = (f32[4,8,128]{2,1,0:T(8,128)S(1)}, f32[4,8,128]{2,1,0:T(8,128)S(1)}, u32[]{:S(2)}, u32[]{:S(2)}) collective-permute-start(f32[4,8,128]{2,1,0:T(8,128)S(1)} %get-tuple-element.57), channel_id=1, source_target_pairs={{0,3},{1,0},{2,1},{3,2},{4,7},{5,4},{6,5},{7,6},{8,11},{9,8},{10,9... | collective-permute-start | bytes 49160 | tf_op jit(solution)/shard_map/ppermute | solution.py:383
